TPU v7x, 128 devices: a whole 4x4x4 slice. The times are simulated.
128 devices in a mesh: req: 8 (over x, y_lo), ctx: 16 (over y_hi, z, core).
Axes of the slice: x: 4, y: 4 (y_hi: 2, y_lo: 2; y = y_hi * 2 + y_lo), z: 4, core: 2. Of those that a mesh axis runs over, the one named last changes fastest.
Arguments:
- cand_feats: bfloat16 [65536, 512], P(('req', 'ctx')), may hold values from -6 to 6
- cand_user: int32 [65536, 1], P(('req', 'ctx')), may hold values from 0 to 7; in each aligned block of 512 rows (0 to 511, 512 to 1023, ...) at most 96 rows name the same one
- history: bfloat16 [8, 2048, 512], P('req', 'ctx'), may hold values from -6 to 6
- hist_len: int32 [8], replicated, may hold values from 128 to 2048, as said below
- hist_bucket: int32 [8, 2048], P('req', 'ctx'), may hold values from 0 to 127
- w_qu: bfloat16 [2, 512, 1024], replicated, may hold values from -0.625 to 0.625
- w_kv: bfloat16 [2, 512, 1024], replicated, may hold values from -0.625 to 0.625
- w_out: bfloat16 [2, 512, 512], replicated, may hold values from -0.25 to 0.25
- bias_table: float32 [2, 8, 128], replicated, may hold values from -9 to -4
- mlp_in: bfloat16 [512, 1024], replicated, may hold values from -0.25 to 0.25
- mlp_out: bfloat16 [1024, 8], replicated, may hold values from -0.1875 to 0.1875
Outputs:
- encoded: bfloat16 [65536, 512], P(('req', 'ctx'))
- task_logits: float32 [65536, 8], P(('req', 'ctx'))
Inputs may be any that keep to these rules, and one draw needn't show every extreme that they name: `cand_user`: in each aligned block of 512 rows (the rows of one device) no user is named by more than 96 rows; in every draw some block names some user exactly 96 times. Events at positions hist_len[u] and later are not part of user u's history; in every draw some user has all 2048 events.
All inputs are finite; a program needn't handle non-finite values.
Results may differ from a plain program's by a relative error of at most 0.015.
Values may be sent and summed in bfloat16 or wider, within the bound.
No kernel may reach another device: no remote copies, remote signals or barrier semaphores. Data moves between devices by JAX's collectives and lax.ppermute only.
A program may use at most 128 MiB of HBM per device.

v0:
```python
import math

import jax
import jax.numpy as jnp
from jax import lax
from jax.sharding import PartitionSpec as P


def layer_norm(values):
    average = jnp.mean(values, axis=-1, keepdims=True)
    centered = values - average
    spread = jnp.mean(centered * centered, axis=-1, keepdims=True)
    return centered * lax.rsqrt(spread + 1e-05)


def attend_block(queries, key_rows, value_rows, key_bias, first_row, hist_length):
    slot_count, feature_width = queries.shape
    head_count = key_bias.shape[1]
    head_size = feature_width // head_count
    query_heads = queries.reshape(slot_count, head_count, head_size)
    key_heads = key_rows.reshape(-1, head_count, head_size)
    value_heads = value_rows.reshape(-1, head_count, head_size)
    scores = jnp.einsum(
        "shd,rhd->hsr", query_heads, key_heads, preferred_element_type=jnp.float32
    ) * head_size ** (-0.5)
    scores = scores + key_bias.astype(jnp.float32).T[:, None, :]
    position = first_row + jnp.arange(key_rows.shape[0], dtype=jnp.int32)
    live_keys = position < hist_length
    weights = jnp.where(live_keys[None, None, :], jax.nn.silu(scores), 0.0).astype(jnp.bfloat16)
    mixed = jnp.einsum("hsr,rhd->shd", weights, value_heads, preferred_element_type=jnp.float32)
    return mixed.reshape(slot_count, feature_width)


def key_blocks(running_sum, queries, key_rows, value_rows, key_bias, hist_length):
    row_count = key_rows.shape[0]
    block_rows = math.gcd(row_count, 512)

    def step_fn(block_index, running):
        offset = (block_index * block_rows).astype(jnp.int32)
        key_part = lax.dynamic_slice_in_dim(key_rows, offset, block_rows, 0)
        value_part = lax.dynamic_slice_in_dim(value_rows, offset, block_rows, 0)
        bias_part = lax.dynamic_slice_in_dim(key_bias, offset, block_rows, 0)
        return running + attend_block(queries, key_part, value_part, bias_part, offset, hist_length)

    return lax.fori_loop(0, row_count // block_rows, step_fn, running_sum)


def shards(
    cand_feats,
    cand_user,
    history,
    hist_len,
    hist_bucket,
    w_qu,
    w_kv,
    w_out,
    bias_table,
    mlp_in,
    mlp_out,
):
    row_count, feature_width = cand_feats.shape
    groups = lax.axis_size("req")
    capacity = 3 * row_count // (2 * groups)
    slot_count = groups * capacity
    layer_count = w_qu.shape[0]
    head_count = bias_table.shape[1]
    bucket_count = bias_table.shape[2]
    owners = cand_user[:, 0]
    members = (owners[:, None] == jnp.arange(groups, dtype=jnp.int32)[None, :]).astype(jnp.int32)
    earlier = jnp.cumsum(members, axis=0) - members
    slot_index = owners * capacity + jnp.sum(earlier * members, axis=1)
    outgoing = jnp.zeros((slot_count, feature_width), jnp.bfloat16).at[slot_index].set(cand_feats)
    incoming = lax.all_to_all(
        outgoing.reshape(groups, capacity, feature_width),
        "req",
        split_axis=0,
        concat_axis=0,
        tiled=True,
    )
    current = incoming.reshape(slot_count, feature_width).astype(jnp.float32)
    hist_length = hist_len[lax.axis_index("req")]
    local_rows = history[0]
    normed_hist = layer_norm(local_rows.astype(jnp.float32)).astype(jnp.bfloat16)
    onehot = (hist_bucket[0][:, None] == jnp.arange(bucket_count, dtype=jnp.int32)[None, :]).astype(
        jnp.float32
    )
    bias_flat = bias_table.reshape(layer_count * head_count, bucket_count)
    bias_all = jnp.dot(onehot, bias_flat.T, precision=lax.Precision.HIGHEST).astype(jnp.bfloat16)
    for layer_index in range(layer_count):
        normed = layer_norm(current).astype(jnp.bfloat16)
        projected = jax.nn.silu(
            jnp.dot(normed, w_qu[layer_index], preferred_element_type=jnp.float32)
        )
        queries = projected[:, :feature_width].astype(jnp.bfloat16)
        gate_part = projected[:, feature_width:]
        empty_sum = jnp.zeros((slot_count, feature_width), jnp.float32)
        low_col = layer_index * head_count
        high_col = (layer_index + 1) * head_count
        key_projected = jax.nn.silu(
            jnp.dot(normed_hist, w_kv[layer_index], preferred_element_type=jnp.float32)
        ).astype(jnp.bfloat16)
        key_rows = key_projected[:, :feature_width]
        value_rows = key_projected[:, feature_width:]
        mixed = key_blocks(
            empty_sum,
            queries,
            lax.all_gather(key_rows, "ctx", axis=0, tiled=True),
            lax.all_gather(value_rows, "ctx", axis=0, tiled=True),
            lax.all_gather(bias_all[:, low_col:high_col], "ctx", axis=0, tiled=True),
            hist_length,
        )
        shaped = (layer_norm(mixed) * gate_part).astype(jnp.bfloat16)
        current = current + jnp.dot(shaped, w_out[layer_index], preferred_element_type=jnp.float32)
    finished = current.astype(jnp.bfloat16)
    returned = lax.all_to_all(
        finished.reshape(groups, capacity, feature_width),
        "req",
        split_axis=0,
        concat_axis=0,
        tiled=True,
    )
    encoded = returned.reshape(slot_count, feature_width)[slot_index]
    normed_out = layer_norm(encoded.astype(jnp.float32)).astype(jnp.bfloat16)
    mlp_hidden = jax.nn.silu(
        jnp.dot(normed_out, mlp_in, preferred_element_type=jnp.float32)
    ).astype(jnp.bfloat16)
    task_logits = jnp.dot(mlp_hidden, mlp_out, preferred_element_type=jnp.float32)
    return (encoded, task_logits)


def solution(mesh):
    in_specs = (
        P(("req", "ctx"), None),
        P(("req", "ctx"), None),
        P("req", "ctx", None),
        P(),
        P("req", "ctx"),
        P(),
        P(),
        P(),
        P(),
        P(),
        P(),
    )
    out_specs = (P(("req", "ctx"), None), P(("req", "ctx"), None))
    return jax.shard_map(shards, mesh=mesh, in_specs=in_specs, out_specs=out_specs, check_vma=False)
```

profile of v0, /device:TPU:0, one launch (start us, length us, event | category | flops | bytes accessed | tf_op | source)
XLA Modules:
  0.0 311.5 jit_solution(15689234721704876270)
XLA Ops:
  15.6 3.8 %scatter_custom_fusion = bf16[768,512]{1,0:T(8,128)(2,1)} fusion(s32[512]{0:T(512)S(1)} %bitcast.168, bf16[512,512]{1,0:T(8,128)(2,1)} %param.15, bf16[]{:T(256)} %constant.135.clone.1), kind=kCustom, calls=%fused_computation.92 | custom fusion | bytes 786944 | tf_op jit(solution)/shard_map/scatter | solution.py:72
  19.4 5.4 %all-to-all-start = ((bf16[8,96,512]{2,1,0:T(8,128)(2,1)}), bf16[8,96,512]{2,1,0:T(8,128)(2,1)S(1)}, u32[]{:S(2)}, u32[]{:S(2)}) async-start(bf16[8,96,512]{2,1,0:T(8,128)(2,1)} %bitcast.6), calls=%async_computation | async-start | bytes 1572864 | tf_op jit(solution)/shard_map/all_to_all | solution.py:73
  26.2 25.4 %all_gather.20 = bf16[2048,8]{0,1:T(8,128)(2,1)S(1)} all-gather(bf16[128,8]{0,1:T(8,128)(2,1)S(1)} %get-tuple-element.365), channel_id=1, replica_groups=mesh['req'=8,'ctx'=16] {'ctx'}, dimensions={0}, use_global_device_ids=true | all-gather | bytes 34816 | tf_op jit(solution)/shard_map/all_gather | solution.py:109
  51.7 20.6 %all_gather.23 = bf16[2048,8]{0,1:T(8,128)(2,1)S(1)} all-gather(bf16[128,8]{0,1:T(8,128)(2,1)S(1)} %get-tuple-element.364), channel_id=1, replica_groups=mesh['req'=8,'ctx'=16] {'ctx'}, dimensions={0}, use_global_device_ids=true | all-gather | bytes 34816 | tf_op jit(solution)/shard_map/all_gather | solution.py:109
  80.5 37.8 %all-gather.7.cloned.1.call-done = bf16[2048,512]{1,0:T(8,128)(2,1)} async-done(((bf16[128,512]{1,0:T(8,128)(2,1)}), bf16[2048,512]{1,0:T(8,128)(2,1)}) %all-gather.7.cloned.1.call-update) | async-done | bytes 2097168 | tf_op jit(solution)/shard_map/all_gather | solution.py:107
  118.3 65.8 %while.28 = (s32[]{:T(128)}, f32[768,512]{0,1:T(8,128)}, bf16[2048,512]{1,0:T(8,128)(2,1)}, s32[]{:T(128)}, bf16[2048,512]{1,0:T(8,128)(2,1)}, /*index=5*/bf16[7...) while((s32[]{:T(128)}, f32[768,512]{0,1:T(8,128)}, ...), condition=%wide.region_9.10_spmd.clone, body=%wide.region_8.9_spmd.clone.sunk | while | flops 831263744 | bytes 12362933 | solution.py:45
  124.0 7.5 %fusion.116 = f32[8,64,768]{2,1,0:T(8,128)} fusion(bf16[512,8,64]{0,2,1:T(8,128)(2,1)} %bitcast.159, f32[8,512]{1,0:T(8,128)S(1)} %convert_bitcast_fusion.5, pred[512]{0:T(512)(128)(4,1)S(1)} %add_compare_fusion.4, bf16[512,8,64]{0,2,1:T(8,128)(2,1)} %bitcast.161, bf16[768,8,64]{0,2,1:T(8,128)(2,1)} %bitcast.164), kind=kOutput, calls=%fused_computation.9.clone.1 | convolution fusion | flops 830472192 | bytes 3424768 | tf_op jit(solution)/shard_map/while/body/eval_jaxpr/hsr,rhd->shd/dot_general | solution.py:30
  131.5 2.8 bitcast_add_fusion.5
  140.1 7.5 %fusion.116 = f32[8,64,768]{2,1,0:T(8,128)} fusion(bf16[512,8,64]{0,2,1:T(8,128)(2,1)} %bitcast.159, f32[8,512]{1,0:T(8,128)S(1)} %convert_bitcast_fusion.5, pred[512]{0:T(512)(128)(4,1)S(1)} %add_compare_fusion.4, bf16[512,8,64]{0,2,1:T(8,128)(2,1)} %bitcast.161, bf16[768,8,64]{0,2,1:T(8,128)(2,1)} %bitcast.164), kind=kOutput, calls=%fused_computation.9.clone.1 | convolution fusion | flops 830472192 | bytes 3424768 | tf_op jit(solution)/shard_map/while/body/eval_jaxpr/hsr,rhd->shd/dot_general | solution.py:30
  147.6 3.3 %bitcast_add_fusion.5 = f32[768,512]{0,1:T(8,128)} fusion(f32[8,64,768]{2,1,0:T(8,128)} %fusion.116, f32[768,512]{0,1:T(8,128)} %get-tuple-element.474, pred[]{:T(512)S(6)} %compare.6), kind=kLoop, calls=%fused_computation.11.clone.1 | loop fusion | flops 786432 | bytes 4718593 | tf_op jit(solution)/shard_map/while/body/eval_jaxpr/add | solution.py:43
  156.6 7.5 %fusion.116 = f32[8,64,768]{2,1,0:T(8,128)} fusion(bf16[512,8,64]{0,2,1:T(8,128)(2,1)} %bitcast.159, f32[8,512]{1,0:T(8,128)S(1)} %convert_bitcast_fusion.5, pred[512]{0:T(512)(128)(4,1)S(1)} %add_compare_fusion.4, bf16[512,8,64]{0,2,1:T(8,128)(2,1)} %bitcast.161, bf16[768,8,64]{0,2,1:T(8,128)(2,1)} %bitcast.164), kind=kOutput, calls=%fused_computation.9.clone.1 | convolution fusion | flops 830472192 | bytes 3424768 | tf_op jit(solution)/shard_map/while/body/eval_jaxpr/hsr,rhd->shd/dot_general | solution.py:30
  164.1 3.4 %bitcast_add_fusion.5 = f32[768,512]{0,1:T(8,128)} fusion(f32[8,64,768]{2,1,0:T(8,128)} %fusion.116, f32[768,512]{0,1:T(8,128)} %get-tuple-element.474, pred[]{:T(512)S(6)} %compare.6), kind=kLoop, calls=%fused_computation.11.clone.1 | loop fusion | flops 786432 | bytes 4718593 | tf_op jit(solution)/shard_map/while/body/eval_jaxpr/add | solution.py:43
  173.3 7.5 %fusion.116 = f32[8,64,768]{2,1,0:T(8,128)} fusion(bf16[512,8,64]{0,2,1:T(8,128)(2,1)} %bitcast.159, f32[8,512]{1,0:T(8,128)S(1)} %convert_bitcast_fusion.5, pred[512]{0:T(512)(128)(4,1)S(1)} %add_compare_fusion.4, bf16[512,8,64]{0,2,1:T(8,128)(2,1)} %bitcast.161, bf16[768,8,64]{0,2,1:T(8,128)(2,1)} %bitcast.164), kind=kOutput, calls=%fused_computation.9.clone.1 | convolution fusion | flops 830472192 | bytes 3424768 | tf_op jit(solution)/shard_map/while/body/eval_jaxpr/hsr,rhd->shd/dot_general | solution.py:30
  180.8 3.3 %bitcast_add_fusion.5 = f32[768,512]{0,1:T(8,128)} fusion(f32[8,64,768]{2,1,0:T(8,128)} %fusion.116, f32[768,512]{0,1:T(8,128)} %get-tuple-element.474, pred[]{:T(512)S(6)} %compare.6), kind=kLoop, calls=%fused_computation.11.clone.1 | loop fusion | flops 786432 | bytes 4718593 | tf_op jit(solution)/shard_map/while/body/eval_jaxpr/add | solution.py:43
  184.0 3.1 %copy.28 = f32[768,512]{1,0:T(8,128)} copy(f32[768,512]{0,1:T(8,128)} %get-tuple-element.250) | data formatting | bytes 3145728 | tf_op jit(solution)/shard_map/while | solution.py:45
  197.8 18.0 %all-gather.9.cloned.1.call-done = bf16[2048,512]{1,0:T(8,128)(2,1)} async-done(((bf16[128,512]{1,0:T(8,128)(2,1)}), bf16[2048,512]{1,0:T(8,128)(2,1)}) %all-gather.9.cloned.1.call-update) | async-done | bytes 2097168 | tf_op jit(solution)/shard_map/all_gather | solution.py:108
  215.8 60.6 %while.29 = (s32[]{:T(128)}, f32[768,512]{0,1:T(8,128)S(1)}, bf16[2048,512]{1,0:T(8,128)(2,1)}, s32[]{:T(128)}, bf16[2048,512]{1,0:T(8,128)(2,1)}, /*index=5*/bf...) while((s32[]{:T(128)}, f32[768,512]{0,1:T(8,128)S(1)}, ...), condition=%wide.region_15.16_spmd.clone, body=%wide.region_14.15_spmd.clone.sunk | while | flops 831263744 | bytes 12362933 | solution.py:45
  221.6 7.5 %fusion.121 = f32[8,64,768]{2,1,0:T(8,128)} fusion(bf16[512,8,64]{0,2,1:T(8,128)(2,1)} %bitcast.160, f32[8,512]{1,0:T(8,128)S(1)} %convert_bitcast_fusion.6, pred[512]{0:T(512)(128)(4,1)S(1)} %add_compare_fusion.5, bf16[512,8,64]{0,2,1:T(8,128)(2,1)} %bitcast.162, bf16[768,8,64]{0,2,1:T(8,128)(2,1)} %bitcast.163), kind=kOutput, calls=%fused_computation.26.clone.1 | convolution fusion | flops 830472192 | bytes 3424768 | tf_op jit(solution)/shard_map/while/body/eval_jaxpr/hsr,rhd->shd/dot_general | solution.py:30
  236.7 7.5 %fusion.121 = f32[8,64,768]{2,1,0:T(8,128)} fusion(bf16[512,8,64]{0,2,1:T(8,128)(2,1)} %bitcast.160, f32[8,512]{1,0:T(8,128)S(1)} %convert_bitcast_fusion.6, pred[512]{0:T(512)(128)(4,1)S(1)} %add_compare_fusion.5, bf16[512,8,64]{0,2,1:T(8,128)(2,1)} %bitcast.162, bf16[768,8,64]{0,2,1:T(8,128)(2,1)} %bitcast.163), kind=kOutput, calls=%fused_computation.26.clone.1 | convolution fusion | flops 830472192 | bytes 3424768 | tf_op jit(solution)/shard_map/while/body/eval_jaxpr/hsr,rhd->shd/dot_general | solution.py:30
  251.9 7.5 %fusion.121 = f32[8,64,768]{2,1,0:T(8,128)} fusion(bf16[512,8,64]{0,2,1:T(8,128)(2,1)} %bitcast.160, f32[8,512]{1,0:T(8,128)S(1)} %convert_bitcast_fusion.6, pred[512]{0:T(512)(128)(4,1)S(1)} %add_compare_fusion.5, bf16[512,8,64]{0,2,1:T(8,128)(2,1)} %bitcast.162, bf16[768,8,64]{0,2,1:T(8,128)(2,1)} %bitcast.163), kind=kOutput, calls=%fused_computation.26.clone.1 | convolution fusion | flops 830472192 | bytes 3424768 | tf_op jit(solution)/shard_map/while/body/eval_jaxpr/hsr,rhd->shd/dot_general | solution.py:30
  267.0 7.5 %fusion.121 = f32[8,64,768]{2,1,0:T(8,128)} fusion(bf16[512,8,64]{0,2,1:T(8,128)(2,1)} %bitcast.160, f32[8,512]{1,0:T(8,128)S(1)} %convert_bitcast_fusion.6, pred[512]{0:T(512)(128)(4,1)S(1)} %add_compare_fusion.5, bf16[512,8,64]{0,2,1:T(8,128)(2,1)} %bitcast.162, bf16[768,8,64]{0,2,1:T(8,128)(2,1)} %bitcast.163), kind=kOutput, calls=%fused_computation.26.clone.1 | convolution fusion | flops 830472192 | bytes 3424768 | tf_op jit(solution)/shard_map/while/body/eval_jaxpr/hsr,rhd->shd/dot_general | solution.py:30
  280.0 3.6 %add_convert_fusion = bf16[768,512]{1,0:T(8,128)(2,1)} fusion(f32[768,512]{1,0:T(8,128)} %copy-done.5, f32[768,1024]{1,0:T(8,128)} %copy-done.7, f32[768,512]{1,0:T(8,128)S(1)} %copy-done.4, f32[768]{0:T(1024)S(1)} %add_rsqrt_fusion, f32[768]{0:T(1024)S(1)} %broadcast_multiply_fusion, bf16[2,512,512]{2,1,0:T(8,128)(2,1)} %param.22), kind=kOutput, calls=%fused_computation.46 | convolution fusion | flops 405012480 | bytes 6035456 | tf_op jit(solution)/shard_map/dot_general | solution.py:113
  283.6 4.3 %all-to-all-start.1 = ((bf16[8,96,512]{2,1,0:T(8,128)(2,1)}), bf16[8,96,512]{2,1,0:T(8,128)(2,1)S(1)}, u32[]{:S(2)}, u32[]{:S(2)}) async-start(bf16[8,96,512]{2,1,0:T(8,128)(2,1)} %bitcast.20), calls=%async_computation.1 | async-start | bytes 1572864 | tf_op jit(solution)/shard_map/all_to_all | solution.py:115
  287.9 12.9 %all-to-all-done.1 = bf16[8,96,512]{2,1,0:T(8,128)(2,1)S(1)} async-done(((bf16[8,96,512]{2,1,0:T(8,128)(2,1)}), bf16[8,96,512]{2,1,0:T(8,128)(2,1)S(1)}, u32[]{:S(2)}, u32[]{:S(2)}) %all-to-all-start.1) | async-done | bytes 786464 | tf_op jit(solution)/shard_map/all_to_all | solution.py:115
  (146 shorter events, 89.4 us)
Async XLA Ops:
  7.2 296.1 %copy-start = (bf16[512,1024]{1,0:T(8,128)(2,1)S(1)}, bf16[512,1024]{1,0:T(8,128)(2,1)}, u32[]{:S(2)}) copy-start(bf16[512,1024]{1,0:T(8,128)(2,1)} %param.24) | copy-start | bytes 3145732
  7.2 73.3 %all-gather.5.cloned.1.call-start = ((), (), s32[]{:S(2)}) async-start(), calls=%async_computation.2 | async-start | bytes 2228224 | tf_op jit(solution)/shard_map/all_gather | solution.py:108
  9.4 3.4 %copy-start.9 = (bf16[1,128,512]{2,1,0:T(8,128)(2,1)S(1)}, bf16[1,128,512]{2,1,0:T(8,128)(2,1)}, u32[]{:S(2)}) copy-start(bf16[1,128,512]{2,1,0:T(8,128)(2,1)} %param.17) | copy-start | bytes 393220
  9.4 3.4 %copy-start.13 = (bf16[2,512,1024]{2,1,0:T(8,128)(2,1)S(1)}, bf16[2,512,1024]{2,1,0:T(8,128)(2,1)}, u32[]{:S(2)}) copy-start(bf16[2,512,1024]{2,1,0:T(8,128)(2,1)} %param.21) | copy-start | bytes 6291460
  12.0 106.2 %all-gather.7.cloned.1.call-start = ((), (), s32[]{:S(2)}) async-start(), calls=%async_computation.3 | async-start | bytes 2228224 | tf_op jit(solution)/shard_map/all_gather | solution.py:107
  12.8 185.0 %all-gather.11.cloned.1.call-start = ((), (), s32[]{:S(2)}) async-start(), calls=%async_computation.5 | async-start | bytes 2228224 | tf_op jit(solution)/shard_map/all_gather | solution.py:107
  13.3 12.1 %copy-start.18 = (s32[8]{0:T(128)S(1)}, s32[8]{0:T(128)}, u32[]{:S(2)}) copy-start(s32[8]{0:T(128)} %param.18) | copy-start | bytes 100
  13.3 12.7 %copy-start.17 = (f32[2,8,128]{2,1,0:T(8,128)S(1)}, f32[2,8,128]{2,1,0:T(8,128)}, u32[]{:S(2)}) copy-start(f32[2,8,128]{2,1,0:T(8,128)} %param.23) | copy-start | bytes 24580
  13.3 12.7 %copy-start.19 = (s32[1,128]{1,0:T(1,128)S(1)}, s32[1,128]{1,0:T(1,128)}, u32[]{:S(2)}) copy-start(s32[1,128]{1,0:T(1,128)} %param.19) | copy-start | bytes 1540
  15.6 9.8 %copy-start.11 = (s32[512,1]{0,1:T(1,128)}, s32[512,1]{0,1:T(1,128)S(1)}, u32[]{:S(2)}) copy-start(s32[512,1]{0,1:T(1,128)S(1)} %compare_select_fusion) | copy-start | bytes 6148
  19.4 52.9 %all-to-all-start = ((bf16[8,96,512]{2,1,0:T(8,128)(2,1)}), bf16[8,96,512]{2,1,0:T(8,128)(2,1)S(1)}, u32[]{:S(2)}, u32[]{:S(2)}) async-start(bf16[8,96,512]{2,1,0:T(8,128)(2,1)} %bitcast.6), calls=%async_computation | async-start | bytes 1572864 | tf_op jit(solution)/shard_map/all_to_all | solution.py:73
  24.8 191.0 %all-gather.9.cloned.1.call-start = ((), (), s32[]{:S(2)}) async-start(), calls=%async_computation.4 | async-start | bytes 2228224 | tf_op jit(solution)/shard_map/all_gather | solution.py:108
  72.3 3.2 %copy-start.1 = (bf16[8,96,512]{2,1,0:T(8,128)(2,1)}, bf16[8,96,512]{2,1,0:T(8,128)(2,1)S(1)}, u32[]{:S(2)}) copy-start(bf16[8,96,512]{2,1,0:T(8,128)(2,1)S(1)} %all-to-all-done) | copy-start | bytes 2359300
  72.3 1.9 copy-start.14
  75.5 1.7 copy-start.8
  187.2 3.5 %copy-start.2 = (bf16[8,96,512]{2,1,0:T(8,128)(2,1)S(1)}, bf16[8,96,512]{2,1,0:T(8,128)(2,1)}, u32[]{:S(2)}) copy-start(bf16[8,96,512]{2,1,0:T(8,128)(2,1)} %copy-done.1) | copy-start | bytes 2359300
  188.8 1.9 copy-start.3
  190.7 2.8 copy-start.15
  193.1 1.8 copy-start.5
  278.1 1.9 copy-start.4
  280.0 7.9 %copy-start.12 = (s32[512,1]{0,1:T(1,128)S(1)}, s32[512,1]{0,1:T(1,128)}, u32[]{:S(2)}) copy-start(s32[512,1]{0,1:T(1,128)} %copy-done.11) | copy-start | bytes 6148
  283.6 17.2 %all-to-all-start.1 = ((bf16[8,96,512]{2,1,0:T(8,128)(2,1)}), bf16[8,96,512]{2,1,0:T(8,128)(2,1)S(1)}, u32[]{:S(2)}, u32[]{:S(2)}) async-start(bf16[8,96,512]{2,1,0:T(8,128)(2,1)} %bitcast.20), calls=%async_computation.1 | async-start | bytes 1572864 | tf_op jit(solution)/shard_map/all_to_all | solution.py:115
  300.8 2.5 copy-start.16
  302.8 2.2 copy-start.6
  (2 other events, 2.9 us)
Sparse Core Ops, SparseCore 0:
  12.1 56.6 all-gather.4
  71.9 46.3 all-gather.6
  120.7 46.3 all-gather.10
  169.4 46.3 all-gather.8
where the time goes:
time: 313 us; the launch traced here: 312 us
  matrix products  73.1 us (23%)
  waiting for transfers between devices  69.9 us (22%)
  local copies, waits for them, and re-layouts  62.6 us (20%)
  blocking collectives  46 us (15%)
  other arithmetic  35.7 us (11%)
  between operations  14.2 us (5%)
  starting transfers between devices  9.83 us (3%)
    dot_general x8, matrix products, attend_block(): jnp.einsum('hsr,rhd->shd', weights, value_heads, preferred_element_type=j...  60.2 us
    all_gather x2, blocking collectives, shards(): lax.all_gather(bias_all[:, low_col:high_col], 'ctx', axis=0, tiled=True)  46 us
    all_gather x2, waiting for transfers between devices, shards(): lax.all_gather(key_rows, 'ctx', axis=0, tiled=True)  37.8 us
    dynamic_slice x16, local copies, waits for them, and re-layouts, step_fn(): key_part = lax.dynamic_slice_in_dim(key_rows, offset, block_rows, 0)  24.5 us
    add x8, other arithmetic, step_fn(): running + attend_block(queries, key_part, value_part, bias_part, offset,...  19.9 us
    all_gather x2, waiting for transfers between devices, shards(): lax.all_gather(value_rows, 'ctx', axis=0, tiled=True)  18 us
    dynamic_slice x8, local copies, waits for them, and re-layouts, step_fn(): value_part = lax.dynamic_slice_in_dim(value_rows, offset, block_rows, 0)  16.4 us
    all_to_all x1, waiting for transfers between devices, shards(): lax.all_to_all(finished.reshape(groups, capacity, feature_width), 'req',...  12.9 us
  transfers between devices with their start and end apart: 6, of which 3 were waited for; matrix products, arithmetic and copies ran while one was open for 29% of the time, Pallas kernels for 0%

commit v1 on v0

v1 whole, which is shorter than its diff:
```python
import functools

import jax
import jax.numpy as jnp
from jax import lax
from jax.experimental import pallas as pl
from jax.experimental.pallas import tpu as pltpu
from jax.sharding import PartitionSpec as P

BF16 = jnp.bfloat16
F32 = jnp.float32
NT = (((1,), (1,)), ((), ()))
TN = (((0,), (0,)), ((), ()))
TT = (((0,), (1,)), ((), ()))
MIB = 2**20
BIAS_ROWS = 16


def dot(left, right, dims=(((1,), (0,)), ((), ()))):
    return lax.dot_general(left, right, dims, preferred_element_type=F32)


def layer_norm(values):
    average = jnp.mean(values, axis=-1, keepdims=True)
    centered = values - average
    spread = jnp.mean(centered * centered, axis=-1, keepdims=True)
    return centered * lax.rsqrt(spread + 1e-05)


def silu_of_half(half):
    return half + half * jnp.tanh(half)


def silu(values):
    return silu_of_half(0.5 * values)


def slots_of(owner_column, groups, capacity):
    rows = owner_column.shape[0]
    members = owner_column == lax.broadcasted_iota(jnp.int32, (rows, groups), 1)
    before = lax.broadcasted_iota(jnp.int32, (rows, rows), 1) < lax.broadcasted_iota(
        jnp.int32, (rows, rows), 0
    )
    earlier = dot(before.astype(BF16), members.astype(BF16))
    base = lax.broadcasted_iota(jnp.int32, (rows, groups), 1).astype(F32) * capacity
    slot = jnp.sum(jnp.where(members, earlier + base, 0.0), axis=1, keepdims=True)
    return slot.astype(jnp.int32)


def dispatch_kernel(groups, capacity, len_ref, feats_ref, owner_ref, hist_ref, bucket_ref, table_ref, out_ref, keys_ref):
    rows = feats_ref.shape[0]
    slot_count = groups * capacity
    slot = slots_of(owner_ref[...], groups, capacity)
    place = (slot == lax.broadcasted_iota(jnp.int32, (rows, slot_count), 1)).astype(BF16)
    out_ref[...] = dot(place, feats_ref[...], TN).astype(BF16)
    key_count = hist_ref.shape[0]
    live = len_ref[lax.axis_index("req")] - lax.axis_index("ctx") * key_count
    normed = layer_norm(hist_ref[...].astype(F32))
    position = lax.broadcasted_iota(jnp.int32, normed.shape, 0)
    keys_ref[:key_count, :] = jnp.where(position < live, normed, 0.0).astype(BF16)
    bucket_count = table_ref.shape[1]
    onehot = lax.broadcasted_iota(jnp.int32, (bucket_count, key_count), 0) == bucket_ref[...]
    bias = dot(table_ref[...].astype(BF16), onehot.astype(BF16))
    keys_ref[key_count:, :] = jnp.zeros((BIAS_ROWS, keys_ref.shape[1]), BF16)
    keys_ref[key_count:, :key_count] = (0.5 * bias).astype(BF16)


def cache_kernel(key_count, heads, keys_ref, w_ref, k_ref, v_ref):
    layers, width = w_ref.shape[0], w_ref.shape[1]
    head_size = width // heads
    normed = keys_ref[:key_count, :]
    bias = keys_ref[key_count:, :key_count]
    row = lax.broadcasted_iota(jnp.int32, (head_size, key_count), 0)
    for layer in range(layers):
        keys = silu(dot(w_ref[layer, :, :width], normed, TT)).astype(BF16)
        values = silu(dot(normed, w_ref[layer, :, width:])).astype(BF16)
        for head in range(heads):
            own = keys[head * head_size : (head + 1) * head_size]
            line = bias[layer * heads + head : layer * heads + head + 1].astype(F32)
            extra = jnp.where(row == 0, line, 0.0).astype(BF16)
            first, second = (own, extra) if head % 2 == 0 else (extra, own)
            k_ref[layer, head, :head_size, :] = first
            k_ref[layer, head, head_size:, :] = second
        for pair in range(heads // 2):
            v_ref[layer, pair] = values[:, pair * 128 : (pair + 1) * 128]


def layers_kernel(block, x_ref, k_ref, v_ref, wq_ref, wo_ref, out_ref, x_buf, q_buf, gate_buf, mixed_buf):
    rows, width = x_ref.shape
    layers, heads, pair_width, _ = k_ref.shape
    half = pair_width // 2
    scale = half**-0.5
    x_buf[...] = x_ref[...].astype(F32)
    for layer in range(layers):
        def project(step, _):
            at = pl.ds(pl.multiple_of(step * block, block), block)
            normed = layer_norm(x_buf[at, :]).astype(BF16)
            projected = silu(dot(normed, wq_ref[layer]))
            gate_buf[at, :] = projected[:, width:]
            queries = projected[:, :width].astype(BF16) * BF16(0.5 * scale)
            lane = lax.broadcasted_iota(jnp.int32, (block, pair_width), 1)
            for pair in range(heads // 2):
                own = queries[:, pair * pair_width : (pair + 1) * pair_width].astype(F32)
                q_buf[2 * pair, at, :] = jnp.where(lane < half, own, jnp.where(lane == half, 1.0, 0.0)).astype(BF16)
                q_buf[2 * pair + 1, at, :] = jnp.where(lane >= half, own, jnp.where(lane == 0, 1.0, 0.0)).astype(BF16)
            return 0

        lax.fori_loop(0, rows // block, project, 0)

        def attend(index, _):
            pair = index // (rows // block)
            at = pl.ds(pl.multiple_of((index % (rows // block)) * block, block), block)
            sums = []
            for side in range(2):
                scores = dot(q_buf[2 * pair + side, at, :], k_ref[layer, 2 * pair + side])
                sums.append(dot(silu_of_half(scores).astype(BF16), v_ref[layer, pair]))
            lane = lax.broadcasted_iota(jnp.int32, sums[0].shape, 1)
            mixed_buf[pair, at, :] = jnp.where(lane < half, sums[0], sums[1])
            return 0

        lax.fori_loop(0, heads // 2 * (rows // block), attend, 0)

        def finish(step, _):
            at = pl.ds(pl.multiple_of(step * block, block), block)
            mixed = jnp.concatenate([mixed_buf[pair, at, :] for pair in range(heads // 2)], axis=1)
            shaped = (layer_norm(mixed) * gate_buf[at, :]).astype(BF16)
            x_buf[at, :] = x_buf[at, :] + dot(shaped, wo_ref[layer])
            return 0

        lax.fori_loop(0, rows // block, finish, 0)
    out_ref[...] = x_buf[...].astype(BF16)


def rank_kernel(groups, capacity, back_ref, owner_ref, in_ref, w_out_ref, encoded_ref, logits_ref):
    rows = owner_ref.shape[0]
    slot_count = groups * capacity
    slot = slots_of(owner_ref[...], groups, capacity)
    place = (slot == lax.broadcasted_iota(jnp.int32, (rows, slot_count), 1)).astype(BF16)
    encoded = dot(place, back_ref[...]).astype(BF16)
    encoded_ref[...] = encoded
    normed = layer_norm(encoded.astype(F32)).astype(BF16)
    hidden = silu(dot(normed, in_ref[...])).astype(BF16)
    logits_ref[...] = dot(hidden, w_out_ref[...])


def params(mib):
    return pltpu.CompilerParams(vmem_limit_bytes=mib * MIB)


def shards(cand_feats, cand_user, history, hist_len, hist_bucket, w_qu, w_kv, w_out, bias_table, mlp_in, mlp_out):
    rows, width = cand_feats.shape
    groups, ctx = lax.axis_size("req"), lax.axis_size("ctx")
    capacity = 3 * rows // (2 * groups)
    slot_count = groups * capacity
    layers, heads, buckets = bias_table.shape
    key_count = history.shape[1]
    smem = pl.BlockSpec(memory_space=pltpu.SMEM)
    vmem = pl.BlockSpec(memory_space=pltpu.VMEM)
    outgoing, own_keys = pl.pallas_call(
        functools.partial(dispatch_kernel, groups, capacity),
        name="dispatch",
        in_specs=[smem] + [vmem] * 5,
        out_shape=(
            jax.ShapeDtypeStruct((slot_count, width), BF16),
            jax.ShapeDtypeStruct((key_count + BIAS_ROWS, width), BF16),
        ),
        compiler_params=params(32),
    )(hist_len, cand_feats, cand_user, history[0], hist_bucket, bias_table.reshape(layers * heads, buckets))

    block_rows = key_count + BIAS_ROWS
    same_core = [[i for i in range(ctx) if i % 2 == side] for side in range(2)]
    near = lax.all_to_all(
        jnp.broadcast_to(own_keys[None], (ctx // 2, block_rows, width)),
        "ctx", split_axis=0, concat_axis=0, tiled=True, axis_index_groups=same_core,
    )
    far = lax.ppermute(near, "ctx", [(i, i ^ 1) for i in range(ctx)])
    incoming = lax.all_to_all(
        outgoing.reshape(groups, capacity, width), "req", split_axis=0, concat_axis=0, tiled=True
    ).reshape(slot_count, width)

    all_keys = ctx * key_count
    blocks = jnp.concatenate([near, far], axis=0)
    cached_k, cached_v = pl.pallas_call(
        functools.partial(cache_kernel, key_count, heads),
        name="cache",
        grid=(ctx,),
        in_specs=[
            pl.BlockSpec((pl.Squeezed(), block_rows, width), lambda i: (i, 0, 0)),
            pl.BlockSpec((layers, width, 2 * width), lambda i: (0, 0, 0)),
        ],
        out_specs=(
            pl.BlockSpec((layers, heads, 128, key_count), lambda i: (0, 0, 0, i)),
            pl.BlockSpec((layers, heads // 2, key_count, 128), lambda i: (0, 0, i, 0)),
        ),
        out_shape=(
            jax.ShapeDtypeStruct((layers, heads, 128, all_keys), BF16),
            jax.ShapeDtypeStruct((layers, heads // 2, all_keys, 128), BF16),
        ),
        compiler_params=params(32),
    )(blocks, w_kv)
    finished = pl.pallas_call(
        functools.partial(layers_kernel, 256),
        name="layers",
        in_specs=[vmem] * 5,
        out_shape=jax.ShapeDtypeStruct((slot_count, width), BF16),
        scratch_shapes=[
            pltpu.VMEM((slot_count, width), F32),
            pltpu.VMEM((heads, slot_count, 128), BF16),
            pltpu.VMEM((slot_count, width), F32),
            pltpu.VMEM((heads // 2, slot_count, 128), F32),
        ],
        compiler_params=params(56),
    )(incoming, cached_k, cached_v, w_qu, w_out)
    returned = lax.all_to_all(
        finished.reshape(groups, capacity, width), "req", split_axis=0, concat_axis=0, tiled=True
    ).reshape(slot_count, width)
    return pl.pallas_call(
        functools.partial(rank_kernel, groups, capacity),
        name="rank",
        in_specs=[vmem] * 4,
        out_shape=(
            jax.ShapeDtypeStruct((rows, width), BF16),
            jax.ShapeDtypeStruct((rows, mlp_out.shape[1]), F32),
        ),
        compiler_params=params(32),
    )(returned, cand_user, mlp_in, mlp_out)


def solution(mesh):
    split = P(("req", "ctx"), None)
    in_specs = (split, split, P("req", "ctx", None), P(), P("req", "ctx"), P(), P(), P(), P(), P(), P())
    return jax.shard_map(shards, mesh=mesh, in_specs=in_specs, out_specs=(split, split), check_vma=False)
```

time: 313 us -> 126 us (0.40)
  matrix products: 73.1 us -> 0 us
  Pallas kernels: 0 us -> 61.7 us
  waiting for transfers between devices: 69.9 us -> 12.3 us
  local copies, waits for them, and re-layouts: 62.6 us -> 13.3 us
  other arithmetic: 35.7 us -> 0.21 us
  blocking collectives: 46 us -> 26.4 us
  between operations: 14.2 us -> 0.72 us
    dot_general x16 -> x0, matrix products: 73.1 us -> none  [the longest x8 60.2 us: attend_block(): jnp.einsum('hsr,rhd->shd', weights, value_heads, preferred_element_type=j...]
    pallas_call x0 -> x4, Pallas kernels: none -> 61.7 us  [the longest x1 44.1 us: shards(): pl.pallas_call(functools.partial(layers_kernel, 256), name='layers', in_s...]
    all_gather x4 -> x0, waiting for transfers between devices: 55.8 us -> none  [the longest x2 37.8 us: shards(): lax.all_gather(key_rows, 'ctx', axis=0, tiled=True)]
    all_gather x2 -> x0, blocking collectives: 46 us -> none  [shards(): lax.all_gather(bias_all[:, low_col:high_col], 'ctx', axis=0, tiled=True)]
    dynamic_slice x25 -> x0, local copies, waits for them, and re-layouts: 41.5 us -> none  [the longest x16 24.5 us: step_fn(): key_part = lax.dynamic_slice_in_dim(key_rows, offset, block_rows, 0)]
    all_to_all x0 -> x1, blocking collectives: none -> 26.4 us  [shards(): lax.all_to_all(jnp.broadcast_to(own_keys[None], (ctx // 2, block_rows, wi...]
    add x8 -> x0, other arithmetic: 19.9 us -> none  [step_fn(): running + attend_block(queries, key_part, value_part, bias_part, offset,...]
    reduce_sum x12 -> x0, other arithmetic: 9.16 us -> none  [the longest x6 5.88 us: layer_norm(): spread = jnp.mean(centered * centered, axis=-1, keepdims=True)]
  transfers between devices with their start and end apart: 6 -> 3, of which waited for: 3 -> 1; matrix products, arithmetic and copies ran while one was open for 29% -> 0% of each run, Pallas kernels for 0% -> 10%
where the time goes in v1:
time: 126 us; the launch traced here: 125 us
  Pallas kernels  61.7 us (49%)
  blocking collectives  26.4 us (21%)
  local copies, waits for them, and re-layouts  13.3 us (11%)
  waiting for transfers between devices  12.3 us (10%)
  starting transfers between devices  10.4 us (8%)
    pallas_call x1, Pallas kernels, shards(): pl.pallas_call(functools.partial(layers_kernel, 256), name='layers', in_s...  44.1 us
    all_to_all x1, blocking collectives, shards(): lax.all_to_all(jnp.broadcast_to(own_keys[None], (ctx // 2, block_rows, wi...  26.4 us
    unnamed x24, local copies, waits for them, and re-layouts  12.5 us
    pallas_call x1, Pallas kernels, shards(): pl.pallas_call(functools.partial(cache_kernel, key_count, heads), name='c...  12.4 us
    all_to_all x1, waiting for transfers between devices, shards(): lax.all_to_all(finished.reshape(groups, capacity, width), 'req', split_ax...  12.3 us
    all_to_all x1, starting transfers between devices, shards(): lax.all_to_all(finished.reshape(groups, capacity, width), 'req', split_ax...  5.83 us
    all_to_all x1, starting transfers between devices, shards(): lax.all_to_all(outgoing.reshape(groups, capacity, width), 'req', split_ax...  4.56 us
    pallas_call x1, Pallas kernels, shards(): pl.pallas_call(functools.partial(rank_kernel, groups, capacity), name='ra...  2.66 us
  transfers between devices with their start and end apart: 3, of which 1 were waited for; matrix products, arithmetic and copies ran while one was open for 0% of the time, Pallas kernels for 10%

profile of v1, /device:TPU:0, one launch (start us, length us, event | category | flops | bytes accessed | tf_op | source)
XLA Modules:
  0.0 125.1 jit_solution(6226355486879139869)
XLA Ops:
  0.6 0.8 copy.13.owner_ref
  1.5 0.0 copy-start.4
  1.5 1.0 copy-done.4
  2.5 0.9 copy-done.5
  3.4 0.7 copy-done.6
  4.1 0.7 copy-done.7
  4.8 0.7 copy-done.8
  5.4 2.6 %dispatch.1 = (bf16[768,512]{1,0:T(8,128)(2,1)}, bf16[144,512]{1,0:T(8,128)(2,1)S(1)}) custom-call(s32[8]{0:T(128)S(1)} %copy-done.7, bf16[512,512]{1,0:T(8,128)(2,1)S(1)} %copy-done.4, s32[512,1]{1,0:T(8,128)S(1)} %copy.13.owner_ref, bf16[128,512]{1,0:T(8,128)(2,1)S(1)} %bitcast.7, s32[1,128]{1,0:T(1,128)S(1)} %copy-done.8, f32[16,128]{1,0:T(8,128)S(1)} %bitcast.8), custom_call_target="tpu_custom_call" | custom-call | tf_op jit(solution)/shard_map/dispatch/pallas_call | solution.py:159
  8.0 0.1 broadcast_in_dim.2
  8.1 26.4 %all_to_all.15 = bf16[8,144,512]{2,1,0:T(8,128)(2,1)S(1)} all-to-all(bf16[8,144,512]{2,1,0:T(8,128)(2,1)S(1)} %broadcast_in_dim.2), channel_id=1, replica_groups={{0,2,4,6,8,10,12,14},{1,3,5,7,9,11,13,15},{16,18,20,22,24,26,28,30},{17..., dimensions={0} | all-to-all | bytes 2359296 | tf_op jit(solution)/shard_map/all_to_all | solution.py:172
  34.5 0.0 collective-permute-start
  34.5 4.6 %all-to-all-start = ((bf16[8,96,512]{2,1,0:T(8,128)(2,1)}), bf16[8,96,512]{2,1,0:T(8,128)(2,1)S(1)}, u32[]{:S(2)}, u32[]{:S(2)}) async-start(bf16[8,96,512]{2,1,0:T(8,128)(2,1)} %bitcast.2), calls=%async_computation | async-start | bytes 1572864 | tf_op jit(solution)/shard_map/all_to_all | solution.py:177
  39.1 0.2 pad_maximum_fusion.keys_ref
  39.3 1.4 %copy-done.2 = bf16[2,512,1024]{2,1,0:T(8,128)(2,1)S(1)} copy-done((bf16[2,512,1024]{2,1,0:T(8,128)(2,1)S(1)}, bf16[2,512,1024]{2,1,0:T(8,128)(2,1)}, u32[]{:S(2)}) %copy-start.2) | copy-done | bytes 2097176
  40.7 12.4 %cache.1 = (bf16[2,8,128,2048]{3,2,1,0:T(8,128)(2,1)S(1)}, bf16[2,4,2048,128]{3,2,1,0:T(8,128)(2,1)S(1)}) custom-call(bf16[16,144,512]{2,1,0:T(8,128)(2,1)S(1)} %pad_maximum_fusion.keys_ref, bf16[2,512,1024]{2,1,0:T(8,128)(2,1)S(1)} %copy-done.2), custom_call_target="tpu_custom_call" | custom-call | tf_op jit(solution)/shard_map/cache/pallas_call | solution.py:183
  53.1 3.2 %copy-done = bf16[2,8,128,2048]{3,2,1,0:T(8,128)(2,1)} copy-done((bf16[2,8,128,2048]{3,2,1,0:T(8,128)(2,1)}, bf16[2,8,128,2048]{3,2,1,0:T(8,128)(2,1)S(1)}, u32[]{:S(2)}) %copy-start) | copy-done | bytes 8388632
  56.3 2.0 %copy-done.1 = bf16[2,4,2048,128]{3,2,1,0:T(8,128)(2,1)} copy-done((bf16[2,4,2048,128]{3,2,1,0:T(8,128)(2,1)}, bf16[2,4,2048,128]{3,2,1,0:T(8,128)(2,1)S(1)}, u32[]{:S(2)}) %copy-start.1) | copy-done | bytes 4194328
  58.3 1.0 copy-done.9
  59.2 44.1 %layers.1 = bf16[768,512]{1,0:T(8,128)(2,1)} custom-call(bf16[768,512]{1,0:T(8,128)(2,1)} %bitcast.9, bf16[2,8,128,2048]{3,2,1,0:T(8,128)(2,1)} %copy-done, bf16[2,4,2048,128]{3,2,1,0:T(8,128)(2,1)} %copy-done.1, bf16[2,512,1024]{2,1,0:T(8,128)(2,1)} %wq_ref.1, bf16[2,512,512]{2,1,0:T(8,128)(2,1)} %wo_ref.1), custom_call_target="tpu_custom_call" | custom-call | tf_op jit(solution)/shard_map/layers/pallas_call | solution.py:201
  103.4 5.8 %all-to-all-start.2 = ((bf16[8,96,512]{2,1,0:T(8,128)(2,1)}), bf16[8,96,512]{2,1,0:T(8,128)(2,1)S(1)}, u32[]{:S(2)}, u32[]{:S(2)}) async-start(bf16[8,96,512]{2,1,0:T(8,128)(2,1)} %bitcast.10), calls=%async_computation.2 | async-start | bytes 1572864 | tf_op jit(solution)/shard_map/all_to_all | solution.py:214
  109.2 0.2 copy.15.w_out_ref
  109.4 12.3 %all-to-all-done.2 = bf16[8,96,512]{2,1,0:T(8,128)(2,1)S(1)} async-done(((bf16[8,96,512]{2,1,0:T(8,128)(2,1)}), bf16[8,96,512]{2,1,0:T(8,128)(2,1)S(1)}, u32[]{:S(2)}, u32[]{:S(2)}) %all-to-all-start.2) | async-done | bytes 786464 | tf_op jit(solution)/shard_map/all_to_all | solution.py:214
  121.7 2.7 %rank.1 = (bf16[512,512]{1,0:T(8,128)(2,1)}, f32[512,8]{1,0:T(8,128)S(1)}) custom-call(bf16[768,512]{1,0:T(8,128)(2,1)S(1)} %bitcast.6, s32[512,1]{1,0:T(8,128)S(1)} %copy.13.owner_ref, bf16[512,1024]{1,0:T(8,128)(2,1)S(1)} %copy-done.3, bf16[1024,8]{1,0:T(8,128)(2,1)S(1)} %copy.15.w_out_ref), custom_call_target="tpu_custom_call" | custom-call | tf_op jit(solution)/shard_map/rank/pallas_call | solution.py:217
  124.3 0.7 copy.16
  (14 shorter events, 0.0 us)
Async XLA Ops:
  1.5 1.0 copy-start.4
  2.5 0.9 copy-start.5
  3.4 0.7 copy-start.6
  4.1 0.7 copy-start.7
  4.8 0.7 copy-start.8
  34.5 4.6 %collective-permute-start = (bf16[8,144,512]{2,1,0:T(8,128)(2,1)S(1)}, bf16[8,144,512]{2,1,0:T(8,128)(2,1)S(1)}, u32[]{:S(2)}, u32[]{:S(2)}) collective-permute-start(bf16[8,144,512]{2,1,0:T(8,128)(2,1)S(1)} %all_to_all.15), channel_id=1, source_target_pairs={{0,1},{1,0},{2,3},{3,2},{4,5},{5,4},{6,7},{7,6},{8,9},{9,8},{10,11... | collective-permute-start | bytes 3538952 | tf_op jit(solution)/shard_map/ppermute | solution.py:176
  34.5 23.8 %all-to-all-start = ((bf16[8,96,512]{2,1,0:T(8,128)(2,1)}), bf16[8,96,512]{2,1,0:T(8,128)(2,1)S(1)}, u32[]{:S(2)}, u32[]{:S(2)}) async-start(bf16[8,96,512]{2,1,0:T(8,128)(2,1)} %bitcast.2), calls=%async_computation | async-start | bytes 1572864 | tf_op jit(solution)/shard_map/all_to_all | solution.py:177
  39.1 1.6 %copy-start.2 = (bf16[2,512,1024]{2,1,0:T(8,128)(2,1)S(1)}, bf16[2,512,1024]{2,1,0:T(8,128)(2,1)}, u32[]{:S(2)}) copy-start(bf16[2,512,1024]{2,1,0:T(8,128)(2,1)} %w_ref.1) | copy-start | bytes 6291460
  53.1 3.2 %copy-start = (bf16[2,8,128,2048]{3,2,1,0:T(8,128)(2,1)}, bf16[2,8,128,2048]{3,2,1,0:T(8,128)(2,1)S(1)}, u32[]{:S(2)}) copy-start(bf16[2,8,128,2048]{3,2,1,0:T(8,128)(2,1)S(1)} %get-tuple-element.8.k_ref) | copy-start | bytes 25165828
  56.3 2.0 %copy-start.1 = (bf16[2,4,2048,128]{3,2,1,0:T(8,128)(2,1)}, bf16[2,4,2048,128]{3,2,1,0:T(8,128)(2,1)S(1)}, u32[]{:S(2)}) copy-start(bf16[2,4,2048,128]{3,2,1,0:T(8,128)(2,1)S(1)} %get-tuple-element.9.v_ref) | copy-start | bytes 12582916
  58.3 1.0 copy-start.9
  59.2 50.0 %copy-start.10 = (bf16[1024,8]{0,1:T(8,128)(2,1)S(1)}, bf16[1024,8]{0,1:T(8,128)(2,1)}, u32[]{:S(2)}) copy-start(bf16[1024,8]{0,1:T(8,128)(2,1)} %param.21) | copy-start | bytes 49156
  103.4 18.3 %copy-start.3 = (bf16[512,1024]{1,0:T(8,128)(2,1)S(1)}, bf16[512,1024]{1,0:T(8,128)(2,1)}, u32[]{:S(2)}) copy-start(bf16[512,1024]{1,0:T(8,128)(2,1)} %in_ref.1) | copy-start | bytes 3145732
  103.4 18.3 %all-to-all-start.2 = ((bf16[8,96,512]{2,1,0:T(8,128)(2,1)}), bf16[8,96,512]{2,1,0:T(8,128)(2,1)S(1)}, u32[]{:S(2)}, u32[]{:S(2)}) async-start(bf16[8,96,512]{2,1,0:T(8,128)(2,1)} %bitcast.10), calls=%async_computation.2 | async-start | bytes 1572864 | tf_op jit(solution)/shard_map/all_to_all | solution.py:214

commit v2 on v1

v2 whole, which is shorter than its diff:
```python
import functools

import jax
import jax.numpy as jnp
from jax import lax
from jax.experimental import pallas as pl
from jax.experimental.pallas import tpu as pltpu
from jax.sharding import PartitionSpec as P

BF16 = jnp.bfloat16
F32 = jnp.float32
NT = (((1,), (1,)), ((), ()))
TN = (((0,), (0,)), ((), ()))
TT = (((0,), (1,)), ((), ()))
MIB = 2**20
BIAS_ROWS = 16


def dot(left, right, dims=(((1,), (0,)), ((), ()))):
    return lax.dot_general(left, right, dims, preferred_element_type=F32)


def layer_norm(values):
    average = jnp.mean(values, axis=-1, keepdims=True)
    centered = values - average
    spread = jnp.mean(centered * centered, axis=-1, keepdims=True)
    return centered * lax.rsqrt(spread + 1e-05)


def silu_of_half(half):
    return half + half * jnp.tanh(half)


def silu(values):
    return silu_of_half(0.5 * values)


def slots_of(owner_row, groups, capacity):
    rows = owner_row.shape[1]
    members = owner_row == lax.broadcasted_iota(jnp.int32, (groups, rows), 0)
    before = lax.broadcasted_iota(jnp.int32, (rows, rows), 0) < lax.broadcasted_iota(
        jnp.int32, (rows, rows), 1
    )
    earlier = dot(members.astype(BF16), before.astype(BF16))
    base = lax.broadcasted_iota(jnp.int32, (groups, rows), 0).astype(F32) * capacity
    return jnp.sum(jnp.where(members, earlier + base, 0.0), axis=0, keepdims=True)


def keys_kernel(len_ref, hist_ref, bucket_ref, table_ref, keys_ref):
    key_count = hist_ref.shape[0]
    live = len_ref[lax.axis_index("req")] - lax.axis_index("ctx") * key_count
    normed = layer_norm(hist_ref[...].astype(F32))
    position = lax.broadcasted_iota(jnp.int32, normed.shape, 0)
    keys_ref[:key_count, :] = jnp.where(position < live, normed, 0.0).astype(BF16)
    bucket_count = table_ref.shape[1]
    onehot = lax.broadcasted_iota(jnp.int32, (bucket_count, key_count), 0) == bucket_ref[...]
    bias = dot(table_ref[...].astype(BF16), onehot.astype(BF16))
    keys_ref[key_count:, :] = jnp.zeros((BIAS_ROWS, keys_ref.shape[1]), BF16)
    keys_ref[key_count:, :key_count] = (0.5 * bias).astype(BF16)


def dispatch_kernel(groups, capacity, feats_ref, owner_ref, out_ref):
    rows = feats_ref.shape[0]
    slot_count = groups * capacity
    slot = slots_of(owner_ref[...], groups, capacity).astype(jnp.int32)
    place = (slot == lax.broadcasted_iota(jnp.int32, (slot_count, rows), 0)).astype(BF16)
    out_ref[...] = dot(place, feats_ref[...]).astype(BF16)


def places_kernel(groups, capacity, owner_ref, place_ref):
    rows, slot_count = place_ref.shape
    slot = slots_of(owner_ref[...], groups, capacity)
    diagonal = lax.broadcasted_iota(jnp.int32, (rows, rows), 0) == lax.broadcasted_iota(
        jnp.int32, (rows, rows), 1
    )
    column = jnp.sum(jnp.where(diagonal, slot, 0.0), axis=1, keepdims=True).astype(jnp.int32)
    place_ref[...] = (column == lax.broadcasted_iota(jnp.int32, (rows, slot_count), 1)).astype(BF16)


def layers_kernel(heads, key_count, chunk_blocks, x_ref, *refs):
    blocks = refs[:chunk_blocks]
    wk_ref, wqu_ref, wo_ref, out_ref, x_buf, k_buf, b_buf, v_buf, q_buf, gate_buf, mixed_buf = refs[chunk_blocks:]
    rows, width = x_ref.shape
    layers = wk_ref.shape[0]
    half = width // heads
    pairs = heads // 2
    scale = BF16(0.5 * half**-0.5)

    pieces = [(ref, i) for ref in blocks for i in range(ref.shape[0])]
    per = 4
    eye = (
        lax.broadcasted_iota(jnp.int32, (BIAS_ROWS, 128), 0) == lax.broadcasted_iota(jnp.int32, (BIAS_ROWS, 128), 1)
    ).astype(BF16)
    for first in range(0, len(pieces), per):
        group = pieces[first : first + per]
        at = slice(first * key_count, (first + per) * key_count)
        normed = jnp.concatenate([ref[i, :key_count, :] for ref, i in group], axis=0)
        bias = jnp.concatenate([ref[i, key_count:, :key_count] for ref, i in group], axis=1)
        b_buf[at, :] = dot(bias, eye, TN).astype(BF16)
        for layer in range(layers):
            keys = silu(dot(normed, wk_ref[layer, :, :width])).astype(BF16)
            for pair in range(pairs):
                k_buf[layer, pair, at, :] = keys[:, pair * 128 : (pair + 1) * 128]
            v_buf[layer, :, at] = silu(dot(wk_ref[layer, :, width:], normed, TT)).astype(BF16)

    x_buf[...] = x_ref[...].astype(F32)
    for layer in range(layers):
        normed = layer_norm(x_buf[...]).astype(BF16)
        for part in range(0, 2 * width, 256):
            projected = silu(dot(wqu_ref[layer, :, part : part + 256], normed, TT))
            if part < width:
                q_buf[part : part + 256, :] = projected.astype(BF16) * scale
            else:
                gate_buf[part - width : part - width + 256, :] = projected

        def attend(pair, _):
            bias = b_buf[...]
            left = jnp.concatenate([k_buf[layer, pair], bias], axis=1)
            for side in range(2):
                head = 2 * pair + side
                own = q_buf[pl.ds(pl.multiple_of(head * half, half), half), :]
                none = jnp.zeros((half, rows), BF16)
                row = lax.broadcasted_iota(jnp.int32, (128, rows), 0)
                pick = (row == layer * heads + head).astype(BF16)
                right = jnp.concatenate([own, none, pick] if side == 0 else [none, own, pick], axis=0)
                weights = silu_of_half(dot(left, right)).astype(BF16)
                at = pl.ds(pl.multiple_of(head * half, half), half)
                mixed_buf[at, :] = dot(v_buf[layer, at, :], weights)
            return 0

        lax.fori_loop(0, pairs, attend, 0)
        mixed = mixed_buf[...]
        centered = mixed - jnp.mean(mixed, axis=0, keepdims=True)
        spread = jnp.mean(centered * centered, axis=0, keepdims=True)
        shaped = (centered * lax.rsqrt(spread + 1e-05) * gate_buf[...]).astype(BF16)
        x_buf[...] = x_buf[...] + dot(shaped, wo_ref[layer], TN)
    out_ref[...] = x_buf[...].astype(BF16)


def rank_kernel(back_ref, place_ref, in_ref, w_out_ref, encoded_ref, logits_ref):
    encoded = dot(place_ref[...], back_ref[...]).astype(BF16)
    encoded_ref[...] = encoded
    normed = layer_norm(encoded.astype(F32)).astype(BF16)
    hidden = silu(dot(normed, in_ref[...])).astype(BF16)
    logits_ref[...] = dot(w_out_ref[...], hidden, NT)


def whole(*shape):
    return pl.BlockSpec(shape, lambda i: (0,) * len(shape))


def params(mib):
    return pltpu.CompilerParams(vmem_limit_bytes=mib * MIB)


def shards(cand_feats, cand_user, history, hist_len, hist_bucket, w_qu, w_kv, w_out, bias_table, mlp_in, mlp_out):
    rows, width = cand_feats.shape
    groups, ctx = lax.axis_size("req"), lax.axis_size("ctx")
    capacity = 3 * rows // (2 * groups)
    slot_count = groups * capacity
    layers, heads, buckets = bias_table.shape
    key_count = history.shape[1]
    smem = pl.BlockSpec(memory_space=pltpu.SMEM)
    vmem = pl.BlockSpec(memory_space=pltpu.VMEM)
    owners = cand_user.reshape(1, rows)
    own_keys = pl.pallas_call(
        keys_kernel,
        name="keys",
        grid=(1,),
        in_specs=[smem, whole(key_count, width), whole(1, key_count), whole(layers * heads, buckets)],
        out_specs=whole(key_count + BIAS_ROWS, width),
        out_shape=jax.ShapeDtypeStruct((key_count + BIAS_ROWS, width), BF16),
        compiler_params=params(60),
    )(hist_len, history[0], hist_bucket, bias_table.reshape(layers * heads, buckets))
    block_rows = key_count + BIAS_ROWS

    def hop(array, dy, dz, dc):
        places = [(y, z, c) for y in range(2) for z in range(ctx // 4) for c in range(2)]
        index = {place: i for i, place in enumerate(places)}
        pairs = [
            (index[y, z, c], index[(y + dy) % 2, (z + dz) % (ctx // 4), (c + dc) % 2]) for y, z, c in places
        ]
        return lax.ppermute(array, "ctx", pairs)

    across = hop(own_keys, 1, 0, 0)
    outgoing = pl.pallas_call(
        functools.partial(dispatch_kernel, groups, capacity),
        name="dispatch",
        grid=(1,),
        in_specs=[whole(rows, width), whole(1, rows)],
        out_specs=whole(slot_count, width),
        out_shape=jax.ShapeDtypeStruct((slot_count, width), BF16),
        compiler_params=params(60),
    )(cand_feats, owners)
    own_keys, outgoing = lax.optimization_barrier((own_keys, outgoing))
    near = jnp.stack([own_keys] + [hop(own_keys, 0, step, 0) for step in (1, 3, 2)])
    incoming = lax.all_to_all(
        outgoing.reshape(groups, capacity, width), "req", split_axis=0, concat_axis=0, tiled=True
    ).reshape(slot_count, width)
    far = jnp.stack([across] + [hop(across, 0, step, 0) for step in (1, 3, 2)])
    blocks = [near, hop(near, 0, 0, 1), far, hop(far, 0, 0, 1)]

    all_keys = ctx * key_count
    finished = pl.pallas_call(
        functools.partial(layers_kernel, heads, key_count, len(blocks)),
        name="layers",
        in_specs=[vmem] * (4 + len(blocks)),
        out_shape=jax.ShapeDtypeStruct((slot_count, width), BF16),
        scratch_shapes=[
            pltpu.VMEM((slot_count, width), F32),
            pltpu.VMEM((layers, heads // 2, all_keys, 128), BF16),
            pltpu.VMEM((all_keys, 128), BF16),
            pltpu.VMEM((layers, width, all_keys), BF16),
            pltpu.VMEM((width, slot_count), BF16),
            pltpu.VMEM((width, slot_count), F32),
            pltpu.VMEM((width, slot_count), F32),
        ],
        compiler_params=params(56),
    )(
        incoming,
        *blocks,
        w_kv,
        w_qu,
        w_out,
    )
    returned = lax.all_to_all(
        finished.reshape(groups, capacity, width), "req", split_axis=0, concat_axis=0, tiled=True
    ).reshape(slot_count, width)
    place = pl.pallas_call(
        functools.partial(places_kernel, groups, capacity),
        name="places",
        grid=(1,),
        in_specs=[whole(1, rows)],
        out_specs=whole(rows, slot_count),
        out_shape=jax.ShapeDtypeStruct((rows, slot_count), BF16),
        compiler_params=params(16),
    )(owners)
    tasks = mlp_out.shape[1]
    encoded, logits = pl.pallas_call(
        rank_kernel,
        name="rank",
        in_specs=[vmem] * 4,
        out_shape=(
            jax.ShapeDtypeStruct((rows, width), BF16),
            jax.ShapeDtypeStruct((tasks, rows), F32),
        ),
        compiler_params=params(16),
    )(returned, place, mlp_in, mlp_out.T)
    return encoded, logits.T


def solution(mesh):
    split = P(("req", "ctx"), None)
    in_specs = (split, split, P("req", "ctx", None), P(), P("req", "ctx"), P(), P(), P(), P(), P(), P())
    return jax.shard_map(shards, mesh=mesh, in_specs=in_specs, out_specs=(split, split), check_vma=False)
```

time: 126 us -> 88.5 us (0.70)
  blocking collectives: 26.4 us -> 0 us
  Pallas kernels: 61.7 us -> 44.3 us
  local copies, waits for them, and re-layouts: 13.3 us -> 1.07 us
  starting transfers between devices: 10.4 us -> 21.9 us
  waiting for transfers between devices: 12.3 us -> 20 us
    all_to_all x1 -> x0, blocking collectives: 26.4 us -> none  [shards(): lax.all_to_all(jnp.broadcast_to(own_keys[None], (ctx // 2, block_rows, wi...]
    pallas_call x3 -> x4, Pallas kernels: 59.2 us -> 41.7 us  [the longest x1 37.1 us: shards(): pl.pallas_call(functools.partial(layers_kernel, heads, key_count, len(blo...]
    ppermute x1 -> x9, starting transfers between devices: 0.01 us -> 13.8 us  [hop(): return lax.ppermute(array, 'ctx', pairs)]
    unnamed x24 -> x16, local copies, waits for them, and re-layouts: 12.5 us -> 1.07 us
    all_to_all x1, waiting for transfers between devices: 0.01 us -> 6.61 us  [shards(): lax.all_to_all(outgoing.reshape(groups, capacity, width), 'req', split_ax...]
    ppermute x1 -> x9, waiting for transfers between devices: 0.01 us -> 2.89 us  [hop(): return lax.ppermute(array, 'ctx', pairs)]
    all_to_all x1, starting transfers between devices: 5.83 us -> 3.68 us  [shards(): lax.all_to_all(finished.reshape(groups, capacity, width), 'req', split_ax...]
    all_to_all x1, waiting for transfers between devices: 12.3 us -> 10.5 us  [shards(): lax.all_to_all(finished.reshape(groups, capacity, width), 'req', split_ax...]
  transfers between devices with their start and end apart: 3 -> 11, of which waited for: 1 -> 4; matrix products, arithmetic and copies ran while one was open for 0% -> 0% of each run, Pallas kernels for 10% -> 3%
where the time goes in v2:
time: 88.5 us; the launch traced here: 88.2 us
  Pallas kernels  44.3 us (50%)
  starting transfers between devices  21.9 us (25%)
  waiting for transfers between devices  20 us (23%)
  local copies, waits for them, and re-layouts  1.07 us (1%)
    pallas_call x1, Pallas kernels, shards(): pl.pallas_call(functools.partial(layers_kernel, heads, key_count, len(blo...  37.1 us
    ppermute x9, starting transfers between devices, hop(): return lax.ppermute(array, 'ctx', pairs)  13.8 us
    all_to_all x1, waiting for transfers between devices, shards(): lax.all_to_all(finished.reshape(groups, capacity, width), 'req', split_ax...  10.5 us
    all_to_all x1, waiting for transfers between devices, shards(): lax.all_to_all(outgoing.reshape(groups, capacity, width), 'req', split_ax...  6.61 us
    all_to_all x1, starting transfers between devices, shards(): lax.all_to_all(outgoing.reshape(groups, capacity, width), 'req', split_ax...  4.42 us
    all_to_all x1, starting transfers between devices, shards(): lax.all_to_all(finished.reshape(groups, capacity, width), 'req', split_ax...  3.68 us
    ppermute x9, waiting for transfers between devices, hop(): return lax.ppermute(array, 'ctx', pairs)  2.89 us
    pallas_call x1, Pallas kernels, shards(): pl.pallas_call(functools.partial(dispatch_kernel, groups, capacity), name...  2.64 us
  transfers between devices with their start and end apart: 11, of which 4 were waited for; matrix products, arithmetic and copies ran while one was open for 0% of the time, Pallas kernels for 3%

profile of v2, /device:TPU:0, one launch (start us, length us, event | category | flops | bytes accessed | tf_op | source)
XLA Modules:
  0.0 88.2 jit_solution(7477178715734380870)
XLA Ops:
  0.6 1.8 %keys.1 = bf16[144,512]{1,0:T(8,128)(2,1)} custom-call(s32[8]{0:T(128)} %len_ref.1, bf16[128,512]{1,0:T(8,128)(2,1)} %bitcast.32, s32[1,128]{1,0:T(1,128)} %bucket_ref.1, f32[16,128]{1,0:T(8,128)} %bitcast.33), custom_call_target="tpu_custom_call" | custom-call | tf_op jit(solution)/shard_map/keys/pallas_call | solution.py:166
  2.4 3.3 %collective-permute-start.4 = (bf16[144,512]{1,0:T(8,128)(2,1)}, bf16[144,512]{1,0:T(8,128)(2,1)S(1)}, u32[]{:S(2)}, u32[]{:S(2)}) collective-permute-start(bf16[144,512]{1,0:T(8,128)(2,1)} %keys.1), channel_id=1, source_target_pairs={{0,8},{1,9},{2,10},{3,11},{4,12},{5,13},{6,14},{7,15},{8,0},{9,1},... | collective-permute-start | bytes 442376 | tf_op jit(solution)/shard_map/ppermute | solution.py:183
  5.7 2.6 %dispatch.1 = bf16[768,512]{1,0:T(8,128)(2,1)} custom-call(bf16[512,512]{1,0:T(8,128)(2,1)} %feats_ref.1, s32[1,512]{1,0:T(1,128)} %bitcast.19), custom_call_target="tpu_custom_call" | custom-call | tf_op jit(solution)/shard_map/dispatch/pallas_call | solution.py:186
  8.4 3.9 %collective-permute-start.2 = (bf16[144,512]{1,0:T(8,128)(2,1)}, bf16[144,512]{1,0:T(8,128)(2,1)S(1)}, u32[]{:S(2)}, u32[]{:S(2)}) collective-permute-start(bf16[144,512]{1,0:T(8,128)(2,1)} %keys.1), channel_id=1, source_target_pairs={{0,4},{1,5},{2,6},{3,7},{4,0},{5,1},{6,2},{7,3},{8,12},{9,13},{10,... | collective-permute-start | bytes 442376 | tf_op jit(solution)/shard_map/ppermute | solution.py:183
  12.2 0.7 collective-permute-start.1
  12.9 1.3 %collective-permute-start = (bf16[144,512]{1,0:T(8,128)(2,1)}, bf16[144,512]{1,0:T(8,128)(2,1)S(1)}, u32[]{:S(2)}, u32[]{:S(2)}) collective-permute-start(bf16[144,512]{1,0:T(8,128)(2,1)} %keys.1), channel_id=1, source_target_pairs={{0,2},{1,3},{2,4},{3,5},{4,6},{5,7},{6,0},{7,1},{8,10},{9,11},{10,... | collective-permute-start | bytes 442376 | tf_op jit(solution)/shard_map/ppermute | solution.py:183
  14.3 1.1 %collective-permute-start.7 = (bf16[144,512]{1,0:T(8,128)(2,1)S(1)}, bf16[144,512]{1,0:T(8,128)(2,1)S(1)}, u32[]{:S(2)}, u32[]{:S(2)}) collective-permute-start(bf16[144,512]{1,0:T(8,128)(2,1)S(1)} %collective-permute-done.4), channel_id=1, source_target_pairs={{0,4},{1,5},{2,6},{3,7},{4,0},{5,1},{6,2},{7,3},{8,12},{9,13},{10,... | collective-permute-start | bytes 442376 | tf_op jit(solution)/shard_map/ppermute | solution.py:183
  15.3 2.6 %collective-permute-start.6 = (bf16[144,512]{1,0:T(8,128)(2,1)S(1)}, bf16[144,512]{1,0:T(8,128)(2,1)S(1)}, u32[]{:S(2)}, u32[]{:S(2)}) collective-permute-start(bf16[144,512]{1,0:T(8,128)(2,1)S(1)} %collective-permute-done.4), channel_id=1, source_target_pairs={{0,6},{1,7},{2,0},{3,1},{4,2},{5,3},{6,4},{7,5},{8,14},{9,15},{10,... | collective-permute-start | bytes 442376 | tf_op jit(solution)/shard_map/ppermute | solution.py:183
  18.0 0.8 collective-permute-start.5
  18.8 4.4 %all-to-all-start = ((bf16[8,96,512]{2,1,0:T(8,128)(2,1)}), bf16[8,96,512]{2,1,0:T(8,128)(2,1)S(1)}, u32[]{:S(2)}, u32[]{:S(2)}) async-start(bf16[8,96,512]{2,1,0:T(8,128)(2,1)} %bitcast.23), calls=%async_computation | async-start | bytes 1572864 | tf_op jit(solution)/shard_map/all_to_all | solution.py:197
  23.2 0.1 pad_maximum_fusion.refs_0_
  23.3 0.1 collective-permute-start.3
  23.4 0.1 collective-permute-done.7
  23.5 2.8 %collective-permute-done.6 = bf16[144,512]{1,0:T(8,128)(2,1)S(1)} collective-permute-done((bf16[144,512]{1,0:T(8,128)(2,1)S(1)}, bf16[144,512]{1,0:T(8,128)(2,1)S(1)}, u32[]{:S(2)}, u32[]{:S(2)}) %collective-permute-start.6) | collective-permute-done | bytes 147488 | tf_op jit(solution)/shard_map/ppermute | solution.py:183
  26.3 0.1 pad_maximum_fusion.1.refs_2_
  26.4 0.1 collective-permute-start.8
  26.5 6.6 %all-to-all-done = bf16[8,96,512]{2,1,0:T(8,128)(2,1)S(1)} async-done(((bf16[8,96,512]{2,1,0:T(8,128)(2,1)}), bf16[8,96,512]{2,1,0:T(8,128)(2,1)S(1)}, u32[]{:S(2)}, u32[]{:S(2)}) %all-to-all-start) | async-done | bytes 786464 | tf_op jit(solution)/shard_map/all_to_all | solution.py:197
  33.1 0.8 copy-done.3
  33.9 0.2 copy-done.6
  34.1 37.1 %layers.1 = bf16[768,512]{1,0:T(8,128)(2,1)} custom-call(bf16[768,512]{1,0:T(8,128)(2,1)} %bitcast.21, bf16[4,144,512]{2,1,0:T(8,128)(2,1)} %copy-done.4, bf16[4,144,512]{2,1,0:T(8,128)(2,1)} %copy-done.6, bf16[4,144,512]{2,1,0:T(8,128)(2,1)} %copy-done.5, bf16[4,144,512]{2,1,0:T(8,128)(2,1)} %collective-permute-done.8.refs_3_, ...), custom_call_target="tpu_custom_call" | custom-call | tf_op jit(solution)/shard_map/layers/pallas_call | solution.py:204
  71.2 3.7 %all-to-all-start.1 = ((bf16[8,96,512]{2,1,0:T(8,128)(2,1)}), bf16[8,96,512]{2,1,0:T(8,128)(2,1)S(1)}, u32[]{:S(2)}, u32[]{:S(2)}) async-start(bf16[8,96,512]{2,1,0:T(8,128)(2,1)} %bitcast.22), calls=%async_computation.1 | async-start | bytes 1572864 | tf_op jit(solution)/shard_map/all_to_all | solution.py:226
  74.9 0.4 places.1.place_ref
  75.3 10.5 %all-to-all-done.1 = bf16[8,96,512]{2,1,0:T(8,128)(2,1)S(1)} async-done(((bf16[8,96,512]{2,1,0:T(8,128)(2,1)}), bf16[8,96,512]{2,1,0:T(8,128)(2,1)S(1)}, u32[]{:S(2)}, u32[]{:S(2)}) %all-to-all-start.1) | async-done | bytes 786464 | tf_op jit(solution)/shard_map/all_to_all | solution.py:226
  85.9 2.4 %rank.1 = (bf16[512,512]{1,0:T(8,128)(2,1)}, f32[8,512]{1,0:T(8,128)}) custom-call(bf16[768,512]{1,0:T(8,128)(2,1)S(1)} %bitcast.17, bf16[512,768]{1,0:T(8,128)(2,1)S(1)} %places.1.place_ref, bf16[512,1024]{1,0:T(8,128)(2,1)S(1)} %copy-done, bf16[8,1024]{1,0:T(8,128)(2,1)S(1)} %bitcast.18), custom_call_target="tpu_custom_call" | custom-call | tf_op jit(solution)/shard_map/rank/pallas_call | solution.py:239
  (21 shorter events, 0.0 us)
Async XLA Ops:
  2.4 20.8 %copy-start.7 = (bf16[144,512]{1,0:T(8,128)(2,1)S(1)}, bf16[144,512]{1,0:T(8,128)(2,1)}, u32[]{:S(2)}) copy-start(bf16[144,512]{1,0:T(8,128)(2,1)} %keys.1) | copy-start | bytes 442372
  2.4 11.8 %collective-permute-start.4 = (bf16[144,512]{1,0:T(8,128)(2,1)}, bf16[144,512]{1,0:T(8,128)(2,1)S(1)}, u32[]{:S(2)}, u32[]{:S(2)}) collective-permute-start(bf16[144,512]{1,0:T(8,128)(2,1)} %keys.1), channel_id=1, source_target_pairs={{0,8},{1,9},{2,10},{3,11},{4,12},{5,13},{6,14},{7,15},{8,0},{9,1},... | collective-permute-start | bytes 442376 | tf_op jit(solution)/shard_map/ppermute | solution.py:183
  8.4 9.6 %collective-permute-start.2 = (bf16[144,512]{1,0:T(8,128)(2,1)}, bf16[144,512]{1,0:T(8,128)(2,1)S(1)}, u32[]{:S(2)}, u32[]{:S(2)}) collective-permute-start(bf16[144,512]{1,0:T(8,128)(2,1)} %keys.1), channel_id=1, source_target_pairs={{0,4},{1,5},{2,6},{3,7},{4,0},{5,1},{6,2},{7,3},{8,12},{9,13},{10,... | collective-permute-start | bytes 442376 | tf_op jit(solution)/shard_map/ppermute | solution.py:183
  12.2 10.9 %collective-permute-start.1 = (bf16[144,512]{1,0:T(8,128)(2,1)}, bf16[144,512]{1,0:T(8,128)(2,1)S(1)}, u32[]{:S(2)}, u32[]{:S(2)}) collective-permute-start(bf16[144,512]{1,0:T(8,128)(2,1)} %keys.1), channel_id=1, source_target_pairs={{0,6},{1,7},{2,0},{3,1},{4,2},{5,3},{6,4},{7,5},{8,14},{9,15},{10,... | collective-permute-start | bytes 442376 | tf_op jit(solution)/shard_map/ppermute | solution.py:183
  12.9 10.2 %collective-permute-start = (bf16[144,512]{1,0:T(8,128)(2,1)}, bf16[144,512]{1,0:T(8,128)(2,1)S(1)}, u32[]{:S(2)}, u32[]{:S(2)}) collective-permute-start(bf16[144,512]{1,0:T(8,128)(2,1)} %keys.1), channel_id=1, source_target_pairs={{0,2},{1,3},{2,4},{3,5},{4,6},{5,7},{6,0},{7,1},{8,10},{9,11},{10,... | collective-permute-start | bytes 442376 | tf_op jit(solution)/shard_map/ppermute | solution.py:183
  14.3 9.2 %collective-permute-start.7 = (bf16[144,512]{1,0:T(8,128)(2,1)S(1)}, bf16[144,512]{1,0:T(8,128)(2,1)S(1)}, u32[]{:S(2)}, u32[]{:S(2)}) collective-permute-start(bf16[144,512]{1,0:T(8,128)(2,1)S(1)} %collective-permute-done.4), channel_id=1, source_target_pairs={{0,4},{1,5},{2,6},{3,7},{4,0},{5,1},{6,2},{7,3},{8,12},{9,13},{10,... | collective-permute-start | bytes 442376 | tf_op jit(solution)/shard_map/ppermute | solution.py:183
  15.3 10.9 %collective-permute-start.6 = (bf16[144,512]{1,0:T(8,128)(2,1)S(1)}, bf16[144,512]{1,0:T(8,128)(2,1)S(1)}, u32[]{:S(2)}, u32[]{:S(2)}) collective-permute-start(bf16[144,512]{1,0:T(8,128)(2,1)S(1)} %collective-permute-done.4), channel_id=1, source_target_pairs={{0,6},{1,7},{2,0},{3,1},{4,2},{5,3},{6,4},{7,5},{8,14},{9,15},{10,... | collective-permute-start | bytes 442376 | tf_op jit(solution)/shard_map/ppermute | solution.py:183
  18.0 8.3 %collective-permute-start.5 = (bf16[144,512]{1,0:T(8,128)(2,1)S(1)}, bf16[144,512]{1,0:T(8,128)(2,1)S(1)}, u32[]{:S(2)}, u32[]{:S(2)}) collective-permute-start(bf16[144,512]{1,0:T(8,128)(2,1)S(1)} %collective-permute-done.4), channel_id=1, source_target_pairs={{0,2},{1,3},{2,4},{3,5},{4,6},{5,7},{6,0},{7,1},{8,10},{9,11},{10,... | collective-permute-start | bytes 442376 | tf_op jit(solution)/shard_map/ppermute | solution.py:183
  18.8 14.3 %all-to-all-start = ((bf16[8,96,512]{2,1,0:T(8,128)(2,1)}), bf16[8,96,512]{2,1,0:T(8,128)(2,1)S(1)}, u32[]{:S(2)}, u32[]{:S(2)}) async-start(bf16[8,96,512]{2,1,0:T(8,128)(2,1)} %bitcast.23), calls=%async_computation | async-start | bytes 1572864 | tf_op jit(solution)/shard_map/all_to_all | solution.py:197
  23.3 9.8 %copy-start.4 = (bf16[4,144,512]{2,1,0:T(8,128)(2,1)}, bf16[4,144,512]{2,1,0:T(8,128)(2,1)S(1)}, u32[]{:S(2)}) copy-start(bf16[4,144,512]{2,1,0:T(8,128)(2,1)S(1)} %pad_maximum_fusion.refs_0_) | copy-start | bytes 1769476
  23.3 9.8 %collective-permute-start.3 = (bf16[4,144,512]{2,1,0:T(8,128)(2,1)S(1)}, bf16[4,144,512]{2,1,0:T(8,128)(2,1)S(1)}, u32[]{:S(2)}, u32[]{:S(2)}) collective-permute-start(bf16[4,144,512]{2,1,0:T(8,128)(2,1)S(1)} %pad_maximum_fusion.refs_0_), channel_id=1, source_target_pairs={{0,1},{1,0},{2,3},{3,2},{4,5},{5,4},{6,7},{7,6},{8,9},{9,8},{10,11... | collective-permute-start | bytes 1769480 | tf_op jit(solution)/shard_map/ppermute | solution.py:183
  26.4 6.7 %copy-start.5 = (bf16[4,144,512]{2,1,0:T(8,128)(2,1)}, bf16[4,144,512]{2,1,0:T(8,128)(2,1)S(1)}, u32[]{:S(2)}) copy-start(bf16[4,144,512]{2,1,0:T(8,128)(2,1)S(1)} %pad_maximum_fusion.1.refs_2_) | copy-start | bytes 1769476
  26.4 6.7 %collective-permute-start.8 = (bf16[4,144,512]{2,1,0:T(8,128)(2,1)S(1)}, bf16[4,144,512]{2,1,0:T(8,128)(2,1)}, u32[]{:S(2)}, u32[]{:S(2)}) collective-permute-start(bf16[4,144,512]{2,1,0:T(8,128)(2,1)S(1)} %pad_maximum_fusion.1.refs_2_), channel_id=1, source_target_pairs={{0,1},{1,0},{2,3},{3,2},{4,5},{5,4},{6,7},{7,6},{8,9},{9,8},{10,11... | collective-permute-start | bytes 1769480 | tf_op jit(solution)/shard_map/ppermute | solution.py:183
  33.1 0.9 copy-start.3
  33.1 1.1 %copy-start.6 = (bf16[4,144,512]{2,1,0:T(8,128)(2,1)}, bf16[4,144,512]{2,1,0:T(8,128)(2,1)S(1)}, u32[]{:S(2)}) copy-start(bf16[4,144,512]{2,1,0:T(8,128)(2,1)S(1)} %collective-permute-done.3.refs_1_) | copy-start | bytes 1769476
  34.1 40.8 %copy-start.2 = (s32[512,1]{0,1:T(1,128)S(1)}, s32[512,1]{0,1:T(1,128)}, u32[]{:S(2)}) copy-start(s32[512,1]{0,1:T(1,128)} %param.12) | copy-start | bytes 6148
  71.2 14.6 %copy-start = (bf16[512,1024]{1,0:T(8,128)(2,1)S(1)}, bf16[512,1024]{1,0:T(8,128)(2,1)}, u32[]{:S(2)}) copy-start(bf16[512,1024]{1,0:T(8,128)(2,1)} %in_ref.1) | copy-start | bytes 3145732
  71.2 14.6 %copy-start.1 = (bf16[1024,8]{0,1:T(8,128)(2,1)S(1)}, bf16[1024,8]{0,1:T(8,128)(2,1)}, u32[]{:S(2)}) copy-start(bf16[1024,8]{0,1:T(8,128)(2,1)} %param.21) | copy-start | bytes 49156
  71.2 14.6 %all-to-all-start.1 = ((bf16[8,96,512]{2,1,0:T(8,128)(2,1)}), bf16[8,96,512]{2,1,0:T(8,128)(2,1)S(1)}, u32[]{:S(2)}, u32[]{:S(2)}) async-start(bf16[8,96,512]{2,1,0:T(8,128)(2,1)} %bitcast.22), calls=%async_computation.1 | async-start | bytes 1572864 | tf_op jit(solution)/shard_map/all_to_all | solution.py:226

commit v3 on v2

--- a/solution.py
+++ b/solution.py
@@ -77,32 +77,50 @@
     place_ref[...] = (column == lax.broadcasted_iota(jnp.int32, (rows, slot_count), 1)).astype(BF16)
 
 
-def layers_kernel(heads, key_count, chunk_blocks, x_ref, *refs):
-    blocks = refs[:chunk_blocks]
-    wk_ref, wqu_ref, wo_ref, out_ref, x_buf, k_buf, b_buf, v_buf, q_buf, gate_buf, mixed_buf = refs[chunk_blocks:]
+def layers_kernel(heads, key_count, chunk_blocks, x_hbm, *refs):
+    blocks_hbm = refs[:chunk_blocks]
+    wk_hbm, wqu_hbm, wo_hbm, out_ref, x_buf, k_buf, b_buf, v_buf, q_buf, gate_buf, mixed_buf = refs[chunk_blocks:-6]
+    x_ref, blocks, wk_ref, wqu_ref, wo_ref, sems = refs[-6:]
     rows, width = x_ref.shape
     layers = wk_ref.shape[0]
+
+    block_copies = [
+        pltpu.make_async_copy(blocks_hbm[i], blocks.at[i], sems.at[i]) for i in range(chunk_blocks)
+    ]
+    wk_copies = [
+        pltpu.make_async_copy(wk_hbm.at[layer], wk_ref.at[layer], sems.at[chunk_blocks + layer])
+        for layer in range(layers)
+    ]
+    x_copy = pltpu.make_async_copy(x_hbm, x_ref, sems.at[chunk_blocks + layers])
+    wqu_copy = pltpu.make_async_copy(wqu_hbm, wqu_ref, sems.at[chunk_blocks + layers + 1])
+    wo_copy = pltpu.make_async_copy(wo_hbm, wo_ref, sems.at[chunk_blocks + layers + 2])
+    for copy in [block_copies[0], *wk_copies, *block_copies[1:], x_copy, wqu_copy, wo_copy]:
+        copy.start()
     half = width // heads
     pairs = heads // 2
     scale = BF16(0.5 * half**-0.5)
 
-    pieces = [(ref, i) for ref in blocks for i in range(ref.shape[0])]
-    per = 4
+    per = blocks.shape[1]
     eye = (
         lax.broadcasted_iota(jnp.int32, (BIAS_ROWS, 128), 0) == lax.broadcasted_iota(jnp.int32, (BIAS_ROWS, 128), 1)
     ).astype(BF16)
-    for first in range(0, len(pieces), per):
-        group = pieces[first : first + per]
-        at = slice(first * key_count, (first + per) * key_count)
-        normed = jnp.concatenate([ref[i, :key_count, :] for ref, i in group], axis=0)
-        bias = jnp.concatenate([ref[i, key_count:, :key_count] for ref, i in group], axis=1)
+    for group in range(chunk_blocks):
+        at = slice(group * per * key_count, (group + 1) * per * key_count)
+        block_copies[group].wait()
+        normed = jnp.concatenate([blocks[group, i, :key_count, :] for i in range(per)], axis=0)
+        bias = jnp.concatenate([blocks[group, i, key_count:, :key_count] for i in range(per)], axis=1)
         b_buf[at, :] = dot(bias, eye, TN).astype(BF16)
         for layer in range(layers):
+            if group == 0:
+                wk_copies[layer].wait()
             keys = silu(dot(normed, wk_ref[layer, :, :width])).astype(BF16)
             for pair in range(pairs):
                 k_buf[layer, pair, at, :] = keys[:, pair * 128 : (pair + 1) * 128]
             v_buf[layer, :, at] = silu(dot(wk_ref[layer, :, width:], normed, TT)).astype(BF16)
 
+    x_copy.wait()
+    wqu_copy.wait()
+    wo_copy.wait()
     x_buf[...] = x_ref[...].astype(F32)
     for layer in range(layers):
         normed = layer_norm(x_buf[...]).astype(BF16)
@@ -204,7 +222,7 @@
     finished = pl.pallas_call(
         functools.partial(layers_kernel, heads, key_count, len(blocks)),
         name="layers",
-        in_specs=[vmem] * (4 + len(blocks)),
+        in_specs=[pl.BlockSpec(memory_space=pl.ANY)] * (4 + len(blocks)),
         out_shape=jax.ShapeDtypeStruct((slot_count, width), BF16),
         scratch_shapes=[
             pltpu.VMEM((slot_count, width), F32),
@@ -214,6 +232,12 @@
             pltpu.VMEM((width, slot_count), BF16),
             pltpu.VMEM((width, slot_count), F32),
             pltpu.VMEM((width, slot_count), F32),
+            pltpu.VMEM((slot_count, width), BF16),
+            pltpu.VMEM((len(blocks), *blocks[0].shape), BF16),
+            pltpu.VMEM(w_kv.shape, BF16),
+            pltpu.VMEM(w_qu.shape, BF16),
+            pltpu.VMEM(w_out.shape, BF16),
+            pltpu.SemaphoreType.DMA((len(blocks) + layers + 3,)),
         ],
         compiler_params=params(56),
     )(

time: 88.5 us -> 87.9 us (level)
  no operation moved by 1% of the time
where the time goes in v3:
time: 87.9 us; the launch traced here: 87.6 us
  Pallas kernels  43.6 us (50%)
  starting transfers between devices  22 us (25%)
  waiting for transfers between devices  20 us (23%)
  local copies, waits for them, and re-layouts  1.08 us (1%)
    pallas_call x1, Pallas kernels, shards(): pl.pallas_call(functools.partial(layers_kernel, heads, key_count, len(blo...  36.4 us
    ppermute x9, starting transfers between devices, hop(): return lax.ppermute(array, 'ctx', pairs)  13.8 us
    all_to_all x1, waiting for transfers between devices, shards(): lax.all_to_all(finished.reshape(groups, capacity, width), 'req', split_ax...  10.5 us
    all_to_all x1, waiting for transfers between devices, shards(): lax.all_to_all(outgoing.reshape(groups, capacity, width), 'req', split_ax...  6.61 us
    all_to_all x1, starting transfers between devices, shards(): lax.all_to_all(outgoing.reshape(groups, capacity, width), 'req', split_ax...  4.42 us
    all_to_all x1, starting transfers between devices, shards(): lax.all_to_all(finished.reshape(groups, capacity, width), 'req', split_ax...  3.69 us
    ppermute x9, waiting for transfers between devices, hop(): return lax.ppermute(array, 'ctx', pairs)  2.89 us
    pallas_call x1, Pallas kernels, shards(): pl.pallas_call(functools.partial(dispatch_kernel, groups, capacity), name...  2.64 us
  transfers between devices with their start and end apart: 11, of which 4 were waited for; matrix products, arithmetic and copies ran while one was open for 0% of the time, Pallas kernels for 3%

profile of v3, /device:TPU:0, one launch (start us, length us, event | category | flops | bytes accessed | tf_op | source)
XLA Modules:
  0.0 87.6 jit_solution(7182360812414642648)
XLA Ops:
  0.6 1.8 %keys.1 = bf16[144,512]{1,0:T(8,128)(2,1)} custom-call(s32[8]{0:T(128)} %len_ref.1, bf16[128,512]{1,0:T(8,128)(2,1)} %bitcast.32, s32[1,128]{1,0:T(1,128)} %bucket_ref.1, f32[16,128]{1,0:T(8,128)} %bitcast.33), custom_call_target="tpu_custom_call" | custom-call | tf_op jit(solution)/shard_map/keys/pallas_call | solution.py:184
  2.4 3.3 %collective-permute-start.4 = (bf16[144,512]{1,0:T(8,128)(2,1)}, bf16[144,512]{1,0:T(8,128)(2,1)S(1)}, u32[]{:S(2)}, u32[]{:S(2)}) collective-permute-start(bf16[144,512]{1,0:T(8,128)(2,1)} %keys.1), channel_id=1, source_target_pairs={{0,8},{1,9},{2,10},{3,11},{4,12},{5,13},{6,14},{7,15},{8,0},{9,1},... | collective-permute-start | bytes 442376 | tf_op jit(solution)/shard_map/ppermute | solution.py:201
  5.7 2.6 %dispatch.1 = bf16[768,512]{1,0:T(8,128)(2,1)} custom-call(bf16[512,512]{1,0:T(8,128)(2,1)} %feats_ref.1, s32[1,512]{1,0:T(1,128)} %bitcast.19), custom_call_target="tpu_custom_call" | custom-call | tf_op jit(solution)/shard_map/dispatch/pallas_call | solution.py:204
  8.4 3.9 %collective-permute-start.2 = (bf16[144,512]{1,0:T(8,128)(2,1)}, bf16[144,512]{1,0:T(8,128)(2,1)S(1)}, u32[]{:S(2)}, u32[]{:S(2)}) collective-permute-start(bf16[144,512]{1,0:T(8,128)(2,1)} %keys.1), channel_id=1, source_target_pairs={{0,4},{1,5},{2,6},{3,7},{4,0},{5,1},{6,2},{7,3},{8,12},{9,13},{10,... | collective-permute-start | bytes 442376 | tf_op jit(solution)/shard_map/ppermute | solution.py:201
  12.2 0.7 collective-permute-start.1
  12.9 1.3 %collective-permute-start = (bf16[144,512]{1,0:T(8,128)(2,1)}, bf16[144,512]{1,0:T(8,128)(2,1)S(1)}, u32[]{:S(2)}, u32[]{:S(2)}) collective-permute-start(bf16[144,512]{1,0:T(8,128)(2,1)} %keys.1), channel_id=1, source_target_pairs={{0,2},{1,3},{2,4},{3,5},{4,6},{5,7},{6,0},{7,1},{8,10},{9,11},{10,... | collective-permute-start | bytes 442376 | tf_op jit(solution)/shard_map/ppermute | solution.py:201
  14.3 1.1 %collective-permute-start.7 = (bf16[144,512]{1,0:T(8,128)(2,1)S(1)}, bf16[144,512]{1,0:T(8,128)(2,1)S(1)}, u32[]{:S(2)}, u32[]{:S(2)}) collective-permute-start(bf16[144,512]{1,0:T(8,128)(2,1)S(1)} %collective-permute-done.4), channel_id=1, source_target_pairs={{0,4},{1,5},{2,6},{3,7},{4,0},{5,1},{6,2},{7,3},{8,12},{9,13},{10,... | collective-permute-start | bytes 442376 | tf_op jit(solution)/shard_map/ppermute | solution.py:201
  15.3 2.6 %collective-permute-start.6 = (bf16[144,512]{1,0:T(8,128)(2,1)S(1)}, bf16[144,512]{1,0:T(8,128)(2,1)S(1)}, u32[]{:S(2)}, u32[]{:S(2)}) collective-permute-start(bf16[144,512]{1,0:T(8,128)(2,1)S(1)} %collective-permute-done.4), channel_id=1, source_target_pairs={{0,6},{1,7},{2,0},{3,1},{4,2},{5,3},{6,4},{7,5},{8,14},{9,15},{10,... | collective-permute-start | bytes 442376 | tf_op jit(solution)/shard_map/ppermute | solution.py:201
  18.0 0.8 collective-permute-start.5
  18.8 4.4 %all-to-all-start = ((bf16[8,96,512]{2,1,0:T(8,128)(2,1)}), bf16[8,96,512]{2,1,0:T(8,128)(2,1)S(1)}, u32[]{:S(2)}, u32[]{:S(2)}) async-start(bf16[8,96,512]{2,1,0:T(8,128)(2,1)} %bitcast.23), calls=%async_computation | async-start | bytes 1572864 | tf_op jit(solution)/shard_map/all_to_all | solution.py:215
  23.2 0.1 pad_maximum_fusion.refs_0_
  23.3 0.1 collective-permute-start.3
  23.4 0.1 collective-permute-done.7
  23.5 2.8 %collective-permute-done.6 = bf16[144,512]{1,0:T(8,128)(2,1)S(1)} collective-permute-done((bf16[144,512]{1,0:T(8,128)(2,1)S(1)}, bf16[144,512]{1,0:T(8,128)(2,1)S(1)}, u32[]{:S(2)}, u32[]{:S(2)}) %collective-permute-start.6) | collective-permute-done | bytes 147488 | tf_op jit(solution)/shard_map/ppermute | solution.py:201
  26.3 0.1 pad_maximum_fusion.1.refs_2_
  26.4 0.1 collective-permute-start.8
  26.5 6.6 %all-to-all-done = bf16[8,96,512]{2,1,0:T(8,128)(2,1)S(1)} async-done(((bf16[8,96,512]{2,1,0:T(8,128)(2,1)}), bf16[8,96,512]{2,1,0:T(8,128)(2,1)S(1)}, u32[]{:S(2)}, u32[]{:S(2)}) %all-to-all-start) | async-done | bytes 786464 | tf_op jit(solution)/shard_map/all_to_all | solution.py:215
  33.1 0.8 copy-done.3
  33.9 0.2 copy-done.6
  34.1 36.4 %layers.1 = bf16[768,512]{1,0:T(8,128)(2,1)} custom-call(bf16[768,512]{1,0:T(8,128)(2,1)} %bitcast.21, bf16[4,144,512]{2,1,0:T(8,128)(2,1)} %copy-done.4, bf16[4,144,512]{2,1,0:T(8,128)(2,1)} %copy-done.6, bf16[4,144,512]{2,1,0:T(8,128)(2,1)} %copy-done.5, bf16[4,144,512]{2,1,0:T(8,128)(2,1)} %collective-permute-done.8.refs_3_, ...), custom_call_target="tpu_custom_call" | custom-call | tf_op jit(solution)/shard_map/layers/pallas_call | solution.py:222
  70.6 3.7 %all-to-all-start.1 = ((bf16[8,96,512]{2,1,0:T(8,128)(2,1)}), bf16[8,96,512]{2,1,0:T(8,128)(2,1)S(1)}, u32[]{:S(2)}, u32[]{:S(2)}) async-start(bf16[8,96,512]{2,1,0:T(8,128)(2,1)} %bitcast.22), calls=%async_computation.1 | async-start | bytes 1572864 | tf_op jit(solution)/shard_map/all_to_all | solution.py:250
  74.3 0.4 places.1.place_ref
  74.7 10.5 %all-to-all-done.1 = bf16[8,96,512]{2,1,0:T(8,128)(2,1)S(1)} async-done(((bf16[8,96,512]{2,1,0:T(8,128)(2,1)}), bf16[8,96,512]{2,1,0:T(8,128)(2,1)S(1)}, u32[]{:S(2)}, u32[]{:S(2)}) %all-to-all-start.1) | async-done | bytes 786464 | tf_op jit(solution)/shard_map/all_to_all | solution.py:250
  85.2 2.4 %rank.1 = (bf16[512,512]{1,0:T(8,128)(2,1)}, f32[8,512]{1,0:T(8,128)}) custom-call(bf16[768,512]{1,0:T(8,128)(2,1)S(1)} %bitcast.17, bf16[512,768]{1,0:T(8,128)(2,1)S(1)} %places.1.place_ref, bf16[512,1024]{1,0:T(8,128)(2,1)S(1)} %copy-done, bf16[8,1024]{1,0:T(8,128)(2,1)S(1)} %bitcast.18), custom_call_target="tpu_custom_call" | custom-call | tf_op jit(solution)/shard_map/rank/pallas_call | solution.py:263
  (21 shorter events, 0.1 us)
Async XLA Ops:
  2.4 20.8 %copy-start.7 = (bf16[144,512]{1,0:T(8,128)(2,1)S(1)}, bf16[144,512]{1,0:T(8,128)(2,1)}, u32[]{:S(2)}) copy-start(bf16[144,512]{1,0:T(8,128)(2,1)} %keys.1) | copy-start | bytes 442372
  2.4 11.8 %collective-permute-start.4 = (bf16[144,512]{1,0:T(8,128)(2,1)}, bf16[144,512]{1,0:T(8,128)(2,1)S(1)}, u32[]{:S(2)}, u32[]{:S(2)}) collective-permute-start(bf16[144,512]{1,0:T(8,128)(2,1)} %keys.1), channel_id=1, source_target_pairs={{0,8},{1,9},{2,10},{3,11},{4,12},{5,13},{6,14},{7,15},{8,0},{9,1},... | collective-permute-start | bytes 442376 | tf_op jit(solution)/shard_map/ppermute | solution.py:201
  8.4 9.6 %collective-permute-start.2 = (bf16[144,512]{1,0:T(8,128)(2,1)}, bf16[144,512]{1,0:T(8,128)(2,1)S(1)}, u32[]{:S(2)}, u32[]{:S(2)}) collective-permute-start(bf16[144,512]{1,0:T(8,128)(2,1)} %keys.1), channel_id=1, source_target_pairs={{0,4},{1,5},{2,6},{3,7},{4,0},{5,1},{6,2},{7,3},{8,12},{9,13},{10,... | collective-permute-start | bytes 442376 | tf_op jit(solution)/shard_map/ppermute | solution.py:201
  12.2 10.9 %collective-permute-start.1 = (bf16[144,512]{1,0:T(8,128)(2,1)}, bf16[144,512]{1,0:T(8,128)(2,1)S(1)}, u32[]{:S(2)}, u32[]{:S(2)}) collective-permute-start(bf16[144,512]{1,0:T(8,128)(2,1)} %keys.1), channel_id=1, source_target_pairs={{0,6},{1,7},{2,0},{3,1},{4,2},{5,3},{6,4},{7,5},{8,14},{9,15},{10,... | collective-permute-start | bytes 442376 | tf_op jit(solution)/shard_map/ppermute | solution.py:201
  12.9 10.2 %collective-permute-start = (bf16[144,512]{1,0:T(8,128)(2,1)}, bf16[144,512]{1,0:T(8,128)(2,1)S(1)}, u32[]{:S(2)}, u32[]{:S(2)}) collective-permute-start(bf16[144,512]{1,0:T(8,128)(2,1)} %keys.1), channel_id=1, source_target_pairs={{0,2},{1,3},{2,4},{3,5},{4,6},{5,7},{6,0},{7,1},{8,10},{9,11},{10,... | collective-permute-start | bytes 442376 | tf_op jit(solution)/shard_map/ppermute | solution.py:201
  14.3 9.2 %collective-permute-start.7 = (bf16[144,512]{1,0:T(8,128)(2,1)S(1)}, bf16[144,512]{1,0:T(8,128)(2,1)S(1)}, u32[]{:S(2)}, u32[]{:S(2)}) collective-permute-start(bf16[144,512]{1,0:T(8,128)(2,1)S(1)} %collective-permute-done.4), channel_id=1, source_target_pairs={{0,4},{1,5},{2,6},{3,7},{4,0},{5,1},{6,2},{7,3},{8,12},{9,13},{10,... | collective-permute-start | bytes 442376 | tf_op jit(solution)/shard_map/ppermute | solution.py:201
  15.3 10.9 %collective-permute-start.6 = (bf16[144,512]{1,0:T(8,128)(2,1)S(1)}, bf16[144,512]{1,0:T(8,128)(2,1)S(1)}, u32[]{:S(2)}, u32[]{:S(2)}) collective-permute-start(bf16[144,512]{1,0:T(8,128)(2,1)S(1)} %collective-permute-done.4), channel_id=1, source_target_pairs={{0,6},{1,7},{2,0},{3,1},{4,2},{5,3},{6,4},{7,5},{8,14},{9,15},{10,... | collective-permute-start | bytes 442376 | tf_op jit(solution)/shard_map/ppermute | solution.py:201
  18.0 8.3 %collective-permute-start.5 = (bf16[144,512]{1,0:T(8,128)(2,1)S(1)}, bf16[144,512]{1,0:T(8,128)(2,1)S(1)}, u32[]{:S(2)}, u32[]{:S(2)}) collective-permute-start(bf16[144,512]{1,0:T(8,128)(2,1)S(1)} %collective-permute-done.4), channel_id=1, source_target_pairs={{0,2},{1,3},{2,4},{3,5},{4,6},{5,7},{6,0},{7,1},{8,10},{9,11},{10,... | collective-permute-start | bytes 442376 | tf_op jit(solution)/shard_map/ppermute | solution.py:201
  18.8 14.3 %all-to-all-start = ((bf16[8,96,512]{2,1,0:T(8,128)(2,1)}), bf16[8,96,512]{2,1,0:T(8,128)(2,1)S(1)}, u32[]{:S(2)}, u32[]{:S(2)}) async-start(bf16[8,96,512]{2,1,0:T(8,128)(2,1)} %bitcast.23), calls=%async_computation | async-start | bytes 1572864 | tf_op jit(solution)/shard_map/all_to_all | solution.py:215
  23.3 9.8 %copy-start.4 = (bf16[4,144,512]{2,1,0:T(8,128)(2,1)}, bf16[4,144,512]{2,1,0:T(8,128)(2,1)S(1)}, u32[]{:S(2)}) copy-start(bf16[4,144,512]{2,1,0:T(8,128)(2,1)S(1)} %pad_maximum_fusion.refs_0_) | copy-start | bytes 1769476
  23.3 9.8 %collective-permute-start.3 = (bf16[4,144,512]{2,1,0:T(8,128)(2,1)S(1)}, bf16[4,144,512]{2,1,0:T(8,128)(2,1)S(1)}, u32[]{:S(2)}, u32[]{:S(2)}) collective-permute-start(bf16[4,144,512]{2,1,0:T(8,128)(2,1)S(1)} %pad_maximum_fusion.refs_0_), channel_id=1, source_target_pairs={{0,1},{1,0},{2,3},{3,2},{4,5},{5,4},{6,7},{7,6},{8,9},{9,8},{10,11... | collective-permute-start | bytes 1769480 | tf_op jit(solution)/shard_map/ppermute | solution.py:201
  26.4 6.7 %copy-start.5 = (bf16[4,144,512]{2,1,0:T(8,128)(2,1)}, bf16[4,144,512]{2,1,0:T(8,128)(2,1)S(1)}, u32[]{:S(2)}) copy-start(bf16[4,144,512]{2,1,0:T(8,128)(2,1)S(1)} %pad_maximum_fusion.1.refs_2_) | copy-start | bytes 1769476
  26.4 6.7 %collective-permute-start.8 = (bf16[4,144,512]{2,1,0:T(8,128)(2,1)S(1)}, bf16[4,144,512]{2,1,0:T(8,128)(2,1)}, u32[]{:S(2)}, u32[]{:S(2)}) collective-permute-start(bf16[4,144,512]{2,1,0:T(8,128)(2,1)S(1)} %pad_maximum_fusion.1.refs_2_), channel_id=1, source_target_pairs={{0,1},{1,0},{2,3},{3,2},{4,5},{5,4},{6,7},{7,6},{8,9},{9,8},{10,11... | collective-permute-start | bytes 1769480 | tf_op jit(solution)/shard_map/ppermute | solution.py:201
  33.1 0.9 %copy-start.3 = (bf16[8,96,512]{2,1,0:T(8,128)(2,1)}, bf16[8,96,512]{2,1,0:T(8,128)(2,1)S(1)}, u32[]{:S(2)}) copy-start(bf16[8,96,512]{2,1,0:T(8,128)(2,1)S(1)} %all-to-all-done) | copy-start | bytes 2359300
  33.1 1.1 %copy-start.6 = (bf16[4,144,512]{2,1,0:T(8,128)(2,1)}, bf16[4,144,512]{2,1,0:T(8,128)(2,1)S(1)}, u32[]{:S(2)}) copy-start(bf16[4,144,512]{2,1,0:T(8,128)(2,1)S(1)} %collective-permute-done.3.refs_1_) | copy-start | bytes 1769476
  34.1 40.1 %copy-start.2 = (s32[512,1]{0,1:T(1,128)S(1)}, s32[512,1]{0,1:T(1,128)}, u32[]{:S(2)}) copy-start(s32[512,1]{0,1:T(1,128)} %param.12) | copy-start | bytes 6148
  70.6 14.7 %copy-start = (bf16[512,1024]{1,0:T(8,128)(2,1)S(1)}, bf16[512,1024]{1,0:T(8,128)(2,1)}, u32[]{:S(2)}) copy-start(bf16[512,1024]{1,0:T(8,128)(2,1)} %in_ref.1) | copy-start | bytes 3145732
  70.6 14.6 %copy-start.1 = (bf16[1024,8]{0,1:T(8,128)(2,1)S(1)}, bf16[1024,8]{0,1:T(8,128)(2,1)}, u32[]{:S(2)}) copy-start(bf16[1024,8]{0,1:T(8,128)(2,1)} %param.21) | copy-start | bytes 49156
  70.6 14.6 %all-to-all-start.1 = ((bf16[8,96,512]{2,1,0:T(8,128)(2,1)}), bf16[8,96,512]{2,1,0:T(8,128)(2,1)S(1)}, u32[]{:S(2)}, u32[]{:S(2)}) async-start(bf16[8,96,512]{2,1,0:T(8,128)(2,1)} %bitcast.22), calls=%async_computation.1 | async-start | bytes 1572864 | tf_op jit(solution)/shard_map/all_to_all | solution.py:250

commit v4 on v3

--- a/solution.py
+++ b/solution.py
@@ -79,7 +79,7 @@
 
 def layers_kernel(heads, key_count, chunk_blocks, x_hbm, *refs):
     blocks_hbm = refs[:chunk_blocks]
-    wk_hbm, wqu_hbm, wo_hbm, out_ref, x_buf, k_buf, b_buf, v_buf, q_buf, gate_buf, mixed_buf = refs[chunk_blocks:-6]
+    wk_hbm, wqu_hbm, wo_hbm, out_hbm, x_buf, k_buf, b_buf, v_buf, q_buf, gate_buf, mixed_buf = refs[chunk_blocks:-6]
     x_ref, blocks, wk_ref, wqu_ref, wo_ref, sems = refs[-6:]
     rows, width = x_ref.shape
     layers = wk_ref.shape[0]
@@ -94,7 +94,7 @@
     x_copy = pltpu.make_async_copy(x_hbm, x_ref, sems.at[chunk_blocks + layers])
     wqu_copy = pltpu.make_async_copy(wqu_hbm, wqu_ref, sems.at[chunk_blocks + layers + 1])
     wo_copy = pltpu.make_async_copy(wo_hbm, wo_ref, sems.at[chunk_blocks + layers + 2])
-    for copy in [block_copies[0], *wk_copies, *block_copies[1:], x_copy, wqu_copy, wo_copy]:
+    for copy in [*block_copies[:2], *wk_copies, *block_copies[2:], x_copy, wqu_copy, wo_copy]:
         copy.start()
     half = width // heads
     pairs = heads // 2
@@ -104,11 +104,13 @@
     eye = (
         lax.broadcasted_iota(jnp.int32, (BIAS_ROWS, 128), 0) == lax.broadcasted_iota(jnp.int32, (BIAS_ROWS, 128), 1)
     ).astype(BF16)
-    for group in range(chunk_blocks):
-        at = slice(group * per * key_count, (group + 1) * per * key_count)
-        block_copies[group].wait()
-        normed = jnp.concatenate([blocks[group, i, :key_count, :] for i in range(per)], axis=0)
-        bias = jnp.concatenate([blocks[group, i, key_count:, :key_count] for i in range(per)], axis=1)
+    for group in range(0, chunk_blocks, 2):
+        at = slice(group * per * key_count, (group + 2) * per * key_count)
+        pieces = [(group + side, i) for side in range(2) for i in range(per)]
+        for side in range(2):
+            block_copies[group + side].wait()
+        normed = jnp.concatenate([blocks[g, i, :key_count, :] for g, i in pieces], axis=0)
+        bias = jnp.concatenate([blocks[g, i, key_count:, :key_count] for g, i in pieces], axis=1)
         b_buf[at, :] = dot(bias, eye, TN).astype(BF16)
         for layer in range(layers):
             if group == 0:
@@ -151,8 +153,17 @@
         centered = mixed - jnp.mean(mixed, axis=0, keepdims=True)
         spread = jnp.mean(centered * centered, axis=0, keepdims=True)
         shaped = (centered * lax.rsqrt(spread + 1e-05) * gate_buf[...]).astype(BF16)
-        x_buf[...] = x_buf[...] + dot(shaped, wo_ref[layer], TN)
-    out_ref[...] = x_buf[...].astype(BF16)
+        if layer + 1 < layers:
+            x_buf[...] = x_buf[...] + dot(shaped, wo_ref[layer], TN)
+    part = 256
+    out_copies = []
+    for first in range(0, rows, part):
+        at = slice(first, first + part)
+        x_ref[at, :] = (x_buf[at, :] + dot(shaped[:, at], wo_ref[layers - 1], TN)).astype(BF16)
+        out_copies.append(pltpu.make_async_copy(x_ref.at[at, :], out_hbm.at[at, :], sems.at[first // part]))
+        out_copies[-1].start()
+    for copy in out_copies:
+        copy.wait()
 
 
 def rank_kernel(back_ref, place_ref, in_ref, w_out_ref, encoded_ref, logits_ref):
@@ -223,6 +234,7 @@
         functools.partial(layers_kernel, heads, key_count, len(blocks)),
         name="layers",
         in_specs=[pl.BlockSpec(memory_space=pl.ANY)] * (4 + len(blocks)),
+        out_specs=pl.BlockSpec(memory_space=pl.ANY),
         out_shape=jax.ShapeDtypeStruct((slot_count, width), BF16),
         scratch_shapes=[
             pltpu.VMEM((slot_count, width), F32),

time: 87.9 us -> 87.8 us (level)
  no operation moved by 1% of the time
where the time goes in v4:
time: 87.8 us; the launch traced here: 87.5 us
  Pallas kernels  43.6 us (50%)
  starting transfers between devices  22 us (25%)
  waiting for transfers between devices  20 us (23%)
  local copies, waits for them, and re-layouts  1.08 us (1%)
    pallas_call x1, Pallas kernels, shards(): pl.pallas_call(functools.partial(layers_kernel, heads, key_count, len(blo...  36.4 us
    ppermute x9, starting transfers between devices, hop(): return lax.ppermute(array, 'ctx', pairs)  13.8 us
    all_to_all x1, waiting for transfers between devices, shards(): lax.all_to_all(finished.reshape(groups, capacity, width), 'req', split_ax...  10.5 us
    all_to_all x1, waiting for transfers between devices, shards(): lax.all_to_all(outgoing.reshape(groups, capacity, width), 'req', split_ax...  6.61 us
    all_to_all x1, starting transfers between devices, shards(): lax.all_to_all(outgoing.reshape(groups, capacity, width), 'req', split_ax...  4.42 us
    all_to_all x1, starting transfers between devices, shards(): lax.all_to_all(finished.reshape(groups, capacity, width), 'req', split_ax...  3.69 us
    ppermute x9, waiting for transfers between devices, hop(): return lax.ppermute(array, 'ctx', pairs)  2.89 us
    pallas_call x1, Pallas kernels, shards(): pl.pallas_call(functools.partial(dispatch_kernel, groups, capacity), name...  2.64 us
  transfers between devices with their start and end apart: 11, of which 4 were waited for; matrix products, arithmetic and copies ran while one was open for 0% of the time, Pallas kernels for 3%

profile of v4, /device:TPU:0, one launch (start us, length us, event | category | flops | bytes accessed | tf_op | source)
XLA Modules:
  0.0 87.5 jit_solution(14750202233040763327)
XLA Ops:
  0.6 1.8 %keys.1 = bf16[144,512]{1,0:T(8,128)(2,1)} custom-call(s32[8]{0:T(128)} %len_ref.1, bf16[128,512]{1,0:T(8,128)(2,1)} %bitcast.32, s32[1,128]{1,0:T(1,128)} %bucket_ref.1, f32[16,128]{1,0:T(8,128)} %bitcast.33), custom_call_target="tpu_custom_call" | custom-call | tf_op jit(solution)/shard_map/keys/pallas_call | solution.py:195
  2.4 3.3 %collective-permute-start.4 = (bf16[144,512]{1,0:T(8,128)(2,1)}, bf16[144,512]{1,0:T(8,128)(2,1)S(1)}, u32[]{:S(2)}, u32[]{:S(2)}) collective-permute-start(bf16[144,512]{1,0:T(8,128)(2,1)} %keys.1), channel_id=1, source_target_pairs={{0,8},{1,9},{2,10},{3,11},{4,12},{5,13},{6,14},{7,15},{8,0},{9,1},... | collective-permute-start | bytes 442376 | tf_op jit(solution)/shard_map/ppermute | solution.py:212
  5.7 2.6 %dispatch.1 = bf16[768,512]{1,0:T(8,128)(2,1)} custom-call(bf16[512,512]{1,0:T(8,128)(2,1)} %feats_ref.1, s32[1,512]{1,0:T(1,128)} %bitcast.19), custom_call_target="tpu_custom_call" | custom-call | tf_op jit(solution)/shard_map/dispatch/pallas_call | solution.py:215
  8.4 3.9 %collective-permute-start.2 = (bf16[144,512]{1,0:T(8,128)(2,1)}, bf16[144,512]{1,0:T(8,128)(2,1)S(1)}, u32[]{:S(2)}, u32[]{:S(2)}) collective-permute-start(bf16[144,512]{1,0:T(8,128)(2,1)} %keys.1), channel_id=1, source_target_pairs={{0,4},{1,5},{2,6},{3,7},{4,0},{5,1},{6,2},{7,3},{8,12},{9,13},{10,... | collective-permute-start | bytes 442376 | tf_op jit(solution)/shard_map/ppermute | solution.py:212
  12.2 0.7 collective-permute-start.1
  12.9 1.3 %collective-permute-start = (bf16[144,512]{1,0:T(8,128)(2,1)}, bf16[144,512]{1,0:T(8,128)(2,1)S(1)}, u32[]{:S(2)}, u32[]{:S(2)}) collective-permute-start(bf16[144,512]{1,0:T(8,128)(2,1)} %keys.1), channel_id=1, source_target_pairs={{0,2},{1,3},{2,4},{3,5},{4,6},{5,7},{6,0},{7,1},{8,10},{9,11},{10,... | collective-permute-start | bytes 442376 | tf_op jit(solution)/shard_map/ppermute | solution.py:212
  14.3 1.1 %collective-permute-start.7 = (bf16[144,512]{1,0:T(8,128)(2,1)S(1)}, bf16[144,512]{1,0:T(8,128)(2,1)S(1)}, u32[]{:S(2)}, u32[]{:S(2)}) collective-permute-start(bf16[144,512]{1,0:T(8,128)(2,1)S(1)} %collective-permute-done.4), channel_id=1, source_target_pairs={{0,4},{1,5},{2,6},{3,7},{4,0},{5,1},{6,2},{7,3},{8,12},{9,13},{10,... | collective-permute-start | bytes 442376 | tf_op jit(solution)/shard_map/ppermute | solution.py:212
  15.3 2.6 %collective-permute-start.6 = (bf16[144,512]{1,0:T(8,128)(2,1)S(1)}, bf16[144,512]{1,0:T(8,128)(2,1)S(1)}, u32[]{:S(2)}, u32[]{:S(2)}) collective-permute-start(bf16[144,512]{1,0:T(8,128)(2,1)S(1)} %collective-permute-done.4), channel_id=1, source_target_pairs={{0,6},{1,7},{2,0},{3,1},{4,2},{5,3},{6,4},{7,5},{8,14},{9,15},{10,... | collective-permute-start | bytes 442376 | tf_op jit(solution)/shard_map/ppermute | solution.py:212
  18.0 0.8 collective-permute-start.5
  18.8 4.4 %all-to-all-start = ((bf16[8,96,512]{2,1,0:T(8,128)(2,1)}), bf16[8,96,512]{2,1,0:T(8,128)(2,1)S(1)}, u32[]{:S(2)}, u32[]{:S(2)}) async-start(bf16[8,96,512]{2,1,0:T(8,128)(2,1)} %bitcast.23), calls=%async_computation | async-start | bytes 1572864 | tf_op jit(solution)/shard_map/all_to_all | solution.py:226
  23.2 0.1 pad_maximum_fusion.refs_0_
  23.3 0.1 collective-permute-start.3
  23.4 0.1 collective-permute-done.7
  23.5 2.8 %collective-permute-done.6 = bf16[144,512]{1,0:T(8,128)(2,1)S(1)} collective-permute-done((bf16[144,512]{1,0:T(8,128)(2,1)S(1)}, bf16[144,512]{1,0:T(8,128)(2,1)S(1)}, u32[]{:S(2)}, u32[]{:S(2)}) %collective-permute-start.6) | collective-permute-done | bytes 147488 | tf_op jit(solution)/shard_map/ppermute | solution.py:212
  26.3 0.1 pad_maximum_fusion.1.refs_2_
  26.4 0.1 collective-permute-start.8
  26.5 6.6 %all-to-all-done = bf16[8,96,512]{2,1,0:T(8,128)(2,1)S(1)} async-done(((bf16[8,96,512]{2,1,0:T(8,128)(2,1)}), bf16[8,96,512]{2,1,0:T(8,128)(2,1)S(1)}, u32[]{:S(2)}, u32[]{:S(2)}) %all-to-all-start) | async-done | bytes 786464 | tf_op jit(solution)/shard_map/all_to_all | solution.py:226
  33.1 0.8 copy-done.3
  33.9 0.2 copy-done.6
  34.1 36.4 %layers.1 = bf16[768,512]{1,0:T(8,128)(2,1)} custom-call(bf16[768,512]{1,0:T(8,128)(2,1)} %bitcast.21, bf16[4,144,512]{2,1,0:T(8,128)(2,1)} %copy-done.4, bf16[4,144,512]{2,1,0:T(8,128)(2,1)} %copy-done.6, bf16[4,144,512]{2,1,0:T(8,128)(2,1)} %copy-done.5, bf16[4,144,512]{2,1,0:T(8,128)(2,1)} %collective-permute-done.8.refs_3_, ...), custom_call_target="tpu_custom_call" | custom-call | tf_op jit(solution)/shard_map/layers/pallas_call | solution.py:233
  70.5 3.7 %all-to-all-start.1 = ((bf16[8,96,512]{2,1,0:T(8,128)(2,1)}), bf16[8,96,512]{2,1,0:T(8,128)(2,1)S(1)}, u32[]{:S(2)}, u32[]{:S(2)}) async-start(bf16[8,96,512]{2,1,0:T(8,128)(2,1)} %bitcast.22), calls=%async_computation.1 | async-start | bytes 1572864 | tf_op jit(solution)/shard_map/all_to_all | solution.py:262
  74.2 0.4 places.1.place_ref
  74.6 10.5 %all-to-all-done.1 = bf16[8,96,512]{2,1,0:T(8,128)(2,1)S(1)} async-done(((bf16[8,96,512]{2,1,0:T(8,128)(2,1)}), bf16[8,96,512]{2,1,0:T(8,128)(2,1)S(1)}, u32[]{:S(2)}, u32[]{:S(2)}) %all-to-all-start.1) | async-done | bytes 786464 | tf_op jit(solution)/shard_map/all_to_all | solution.py:262
  85.2 2.4 %rank.1 = (bf16[512,512]{1,0:T(8,128)(2,1)}, f32[8,512]{1,0:T(8,128)}) custom-call(bf16[768,512]{1,0:T(8,128)(2,1)S(1)} %bitcast.17, bf16[512,768]{1,0:T(8,128)(2,1)S(1)} %places.1.place_ref, bf16[512,1024]{1,0:T(8,128)(2,1)S(1)} %copy-done, bf16[8,1024]{1,0:T(8,128)(2,1)S(1)} %bitcast.18), custom_call_target="tpu_custom_call" | custom-call | tf_op jit(solution)/shard_map/rank/pallas_call | solution.py:275
  (21 shorter events, 0.1 us)
Async XLA Ops:
  2.4 20.8 %copy-start.7 = (bf16[144,512]{1,0:T(8,128)(2,1)S(1)}, bf16[144,512]{1,0:T(8,128)(2,1)}, u32[]{:S(2)}) copy-start(bf16[144,512]{1,0:T(8,128)(2,1)} %keys.1) | copy-start | bytes 442372
  2.4 11.8 %collective-permute-start.4 = (bf16[144,512]{1,0:T(8,128)(2,1)}, bf16[144,512]{1,0:T(8,128)(2,1)S(1)}, u32[]{:S(2)}, u32[]{:S(2)}) collective-permute-start(bf16[144,512]{1,0:T(8,128)(2,1)} %keys.1), channel_id=1, source_target_pairs={{0,8},{1,9},{2,10},{3,11},{4,12},{5,13},{6,14},{7,15},{8,0},{9,1},... | collective-permute-start | bytes 442376 | tf_op jit(solution)/shard_map/ppermute | solution.py:212
  8.4 9.6 %collective-permute-start.2 = (bf16[144,512]{1,0:T(8,128)(2,1)}, bf16[144,512]{1,0:T(8,128)(2,1)S(1)}, u32[]{:S(2)}, u32[]{:S(2)}) collective-permute-start(bf16[144,512]{1,0:T(8,128)(2,1)} %keys.1), channel_id=1, source_target_pairs={{0,4},{1,5},{2,6},{3,7},{4,0},{5,1},{6,2},{7,3},{8,12},{9,13},{10,... | collective-permute-start | bytes 442376 | tf_op jit(solution)/shard_map/ppermute | solution.py:212
  12.2 10.9 %collective-permute-start.1 = (bf16[144,512]{1,0:T(8,128)(2,1)}, bf16[144,512]{1,0:T(8,128)(2,1)S(1)}, u32[]{:S(2)}, u32[]{:S(2)}) collective-permute-start(bf16[144,512]{1,0:T(8,128)(2,1)} %keys.1), channel_id=1, source_target_pairs={{0,6},{1,7},{2,0},{3,1},{4,2},{5,3},{6,4},{7,5},{8,14},{9,15},{10,... | collective-permute-start | bytes 442376 | tf_op jit(solution)/shard_map/ppermute | solution.py:212
  12.9 10.2 %collective-permute-start = (bf16[144,512]{1,0:T(8,128)(2,1)}, bf16[144,512]{1,0:T(8,128)(2,1)S(1)}, u32[]{:S(2)}, u32[]{:S(2)}) collective-permute-start(bf16[144,512]{1,0:T(8,128)(2,1)} %keys.1), channel_id=1, source_target_pairs={{0,2},{1,3},{2,4},{3,5},{4,6},{5,7},{6,0},{7,1},{8,10},{9,11},{10,... | collective-permute-start | bytes 442376 | tf_op jit(solution)/shard_map/ppermute | solution.py:212
  14.3 9.2 %collective-permute-start.7 = (bf16[144,512]{1,0:T(8,128)(2,1)S(1)}, bf16[144,512]{1,0:T(8,128)(2,1)S(1)}, u32[]{:S(2)}, u32[]{:S(2)}) collective-permute-start(bf16[144,512]{1,0:T(8,128)(2,1)S(1)} %collective-permute-done.4), channel_id=1, source_target_pairs={{0,4},{1,5},{2,6},{3,7},{4,0},{5,1},{6,2},{7,3},{8,12},{9,13},{10,... | collective-permute-start | bytes 442376 | tf_op jit(solution)/shard_map/ppermute | solution.py:212
  15.3 10.9 %collective-permute-start.6 = (bf16[144,512]{1,0:T(8,128)(2,1)S(1)}, bf16[144,512]{1,0:T(8,128)(2,1)S(1)}, u32[]{:S(2)}, u32[]{:S(2)}) collective-permute-start(bf16[144,512]{1,0:T(8,128)(2,1)S(1)} %collective-permute-done.4), channel_id=1, source_target_pairs={{0,6},{1,7},{2,0},{3,1},{4,2},{5,3},{6,4},{7,5},{8,14},{9,15},{10,... | collective-permute-start | bytes 442376 | tf_op jit(solution)/shard_map/ppermute | solution.py:212
  18.0 8.3 %collective-permute-start.5 = (bf16[144,512]{1,0:T(8,128)(2,1)S(1)}, bf16[144,512]{1,0:T(8,128)(2,1)S(1)}, u32[]{:S(2)}, u32[]{:S(2)}) collective-permute-start(bf16[144,512]{1,0:T(8,128)(2,1)S(1)} %collective-permute-done.4), channel_id=1, source_target_pairs={{0,2},{1,3},{2,4},{3,5},{4,6},{5,7},{6,0},{7,1},{8,10},{9,11},{10,... | collective-permute-start | bytes 442376 | tf_op jit(solution)/shard_map/ppermute | solution.py:212
  18.8 14.3 %all-to-all-start = ((bf16[8,96,512]{2,1,0:T(8,128)(2,1)}), bf16[8,96,512]{2,1,0:T(8,128)(2,1)S(1)}, u32[]{:S(2)}, u32[]{:S(2)}) async-start(bf16[8,96,512]{2,1,0:T(8,128)(2,1)} %bitcast.23), calls=%async_computation | async-start | bytes 1572864 | tf_op jit(solution)/shard_map/all_to_all | solution.py:226
  23.3 9.8 %copy-start.4 = (bf16[4,144,512]{2,1,0:T(8,128)(2,1)}, bf16[4,144,512]{2,1,0:T(8,128)(2,1)S(1)}, u32[]{:S(2)}) copy-start(bf16[4,144,512]{2,1,0:T(8,128)(2,1)S(1)} %pad_maximum_fusion.refs_0_) | copy-start | bytes 1769476
  23.3 9.8 %collective-permute-start.3 = (bf16[4,144,512]{2,1,0:T(8,128)(2,1)S(1)}, bf16[4,144,512]{2,1,0:T(8,128)(2,1)S(1)}, u32[]{:S(2)}, u32[]{:S(2)}) collective-permute-start(bf16[4,144,512]{2,1,0:T(8,128)(2,1)S(1)} %pad_maximum_fusion.refs_0_), channel_id=1, source_target_pairs={{0,1},{1,0},{2,3},{3,2},{4,5},{5,4},{6,7},{7,6},{8,9},{9,8},{10,11... | collective-permute-start | bytes 1769480 | tf_op jit(solution)/shard_map/ppermute | solution.py:212
  26.4 6.7 %copy-start.5 = (bf16[4,144,512]{2,1,0:T(8,128)(2,1)}, bf16[4,144,512]{2,1,0:T(8,128)(2,1)S(1)}, u32[]{:S(2)}) copy-start(bf16[4,144,512]{2,1,0:T(8,128)(2,1)S(1)} %pad_maximum_fusion.1.refs_2_) | copy-start | bytes 1769476
  26.4 6.7 %collective-permute-start.8 = (bf16[4,144,512]{2,1,0:T(8,128)(2,1)S(1)}, bf16[4,144,512]{2,1,0:T(8,128)(2,1)}, u32[]{:S(2)}, u32[]{:S(2)}) collective-permute-start(bf16[4,144,512]{2,1,0:T(8,128)(2,1)S(1)} %pad_maximum_fusion.1.refs_2_), channel_id=1, source_target_pairs={{0,1},{1,0},{2,3},{3,2},{4,5},{5,4},{6,7},{7,6},{8,9},{9,8},{10,11... | collective-permute-start | bytes 1769480 | tf_op jit(solution)/shard_map/ppermute | solution.py:212
  33.1 0.9 %copy-start.3 = (bf16[8,96,512]{2,1,0:T(8,128)(2,1)}, bf16[8,96,512]{2,1,0:T(8,128)(2,1)S(1)}, u32[]{:S(2)}) copy-start(bf16[8,96,512]{2,1,0:T(8,128)(2,1)S(1)} %all-to-all-done) | copy-start | bytes 2359300
  33.1 1.1 %copy-start.6 = (bf16[4,144,512]{2,1,0:T(8,128)(2,1)}, bf16[4,144,512]{2,1,0:T(8,128)(2,1)S(1)}, u32[]{:S(2)}) copy-start(bf16[4,144,512]{2,1,0:T(8,128)(2,1)S(1)} %collective-permute-done.3.refs_1_) | copy-start | bytes 1769476
  34.1 40.1 %copy-start.2 = (s32[512,1]{0,1:T(1,128)S(1)}, s32[512,1]{0,1:T(1,128)}, u32[]{:S(2)}) copy-start(s32[512,1]{0,1:T(1,128)} %param.12) | copy-start | bytes 6148
  70.5 14.7 %copy-start = (bf16[512,1024]{1,0:T(8,128)(2,1)S(1)}, bf16[512,1024]{1,0:T(8,128)(2,1)}, u32[]{:S(2)}) copy-start(bf16[512,1024]{1,0:T(8,128)(2,1)} %in_ref.1) | copy-start | bytes 3145732
  70.5 14.7 %copy-start.1 = (bf16[1024,8]{0,1:T(8,128)(2,1)S(1)}, bf16[1024,8]{0,1:T(8,128)(2,1)}, u32[]{:S(2)}) copy-start(bf16[1024,8]{0,1:T(8,128)(2,1)} %param.21) | copy-start | bytes 49156
  70.5 14.6 %all-to-all-start.1 = ((bf16[8,96,512]{2,1,0:T(8,128)(2,1)}), bf16[8,96,512]{2,1,0:T(8,128)(2,1)S(1)}, u32[]{:S(2)}, u32[]{:S(2)}) async-start(bf16[8,96,512]{2,1,0:T(8,128)(2,1)} %bitcast.22), calls=%async_computation.1 | async-start | bytes 1572864 | tf_op jit(solution)/shard_map/all_to_all | solution.py:262
